TPU v7x, 128 devices: a whole 4x4x4 slice. The times are simulated.
128 devices in a mesh: path: 64 (over x, y_lo, z, core), dp: 2 (over y_hi).
Axes of the slice: x: 4, y: 4 (y_hi: 2, y_lo: 2; y = y_hi * 2 + y_lo), z: 4, core: 2. Of those that a mesh axis runs over, the one named last changes fastest.
Arguments:
- activations: bfloat16 [64, 768, 1024], P('path', 'dp'), may hold values from -6 to 6
- cotangent: bfloat16 [64, 768, 1024], P('path', 'dp'), may hold values from -6 to 6
- token_ids: int32 [64, 768], P('path', 'dp'), may hold values from 0 to 31999, as said below
- path_table: int32 [64, 2], replicated, may hold values from 0 to 7
- up_master: float32 [8, 1024, 4096], P(None, 'path', 'dp'), may hold values from -6 to 6
- down_master: float32 [8, 4096, 1024], P(None, 'path', 'dp'), may hold values from -6 to 6
- up_momentum: float32 [8, 1024, 4096], P(None, 'path', 'dp'), may hold values from -3 to 3
- down_momentum: float32 [8, 4096, 1024], P(None, 'path', 'dp'), may hold values from -3 to 3
- up_first: bfloat16 [64, 1024, 4096], P('path', None, 'dp'), may hold values from -0.001953125 to 0.001953125
- up_second: bfloat16 [64, 1024, 4096], P('path', None, 'dp'), may hold values from 3.237801e-10 to 1.169974e-08
- down_first: bfloat16 [64, 4096, 1024], P('path', None, 'dp'), may hold values from -0.001953125 to 0.001953125
- down_second: bfloat16 [64, 4096, 1024], P('path', None, 'dp'), may hold values from 3.237801e-10 to 1.169974e-08
Outputs:
- new_up_master: float32 [8, 1024, 4096], P(None, 'path', 'dp')
- new_down_master: float32 [8, 4096, 1024], P(None, 'path', 'dp')
- new_up_momentum: float32 [8, 1024, 4096], P(None, 'path', 'dp')
- new_down_momentum: float32 [8, 4096, 1024], P(None, 'path', 'dp')
Inputs may be any that keep to these rules, and one draw needn't show every extreme that they name: `token_ids`: in each path's row the ids are nonzero up to a length of at least 192 tokens and 0 (padding) after it. path_table[p, l] is the module of level l that path p uses; a module may be used by no path.
All inputs are finite; a program needn't handle non-finite values.
Results may differ from a plain program's by a relative error of at most 0.0075.
Values may be sent and summed in bfloat16 or wider, within the bound.
A program may use at most 192 MiB of HBM per device.

v0:
```python
import jax
import jax.numpy as jnp
from jax import lax
from jax.sharding import PartitionSpec as P

D = 1024
F = 4096
C = 8


def inner_update(weights, gradient, first_moment, second_moment):
    first_new = 0.9 * first_moment.astype(jnp.float32) + 0.1 * gradient
    second_new = 0.95 * second_moment.astype(jnp.float32) + 0.05 * gradient * gradient
    direction = first_new / (jnp.sqrt(second_new) + 1e-08) + 0.1 * weights.astype(jnp.float32)
    return (0.1 * direction).astype(jnp.bfloat16)


def shards(
    activations,
    cotangent,
    token_ids,
    path_table,
    up_master,
    down_master,
    up_momentum,
    down_momentum,
    up_first,
    up_second,
    down_first,
    down_second,
):
    up_scale = D ** (-0.5)
    down_scale = F ** (-0.5)
    path_count = lax.axis_size("path")
    up_choice = path_table[:, 0]
    down_choice = path_table[:, 1]
    up_cast = up_master.astype(jnp.bfloat16)
    down_cast = down_master.astype(jnp.bfloat16)
    up_pick = jnp.take(up_cast, up_choice, axis=0)
    down_pick = jnp.take(down_cast, down_choice, axis=0)
    up_half, down_half = (
        lax.all_to_all(up_pick, "path", split_axis=0, concat_axis=1, tiled=True),
        lax.all_to_all(down_pick, "path", split_axis=0, concat_axis=1, tiled=True),
    )
    live_mask = (token_ids[0] != 0).astype(jnp.float32)
    live_count = lax.psum(jnp.sum(live_mask), "dp")
    tokens_wide = activations[0].astype(jnp.float32)
    mean_square = jnp.mean(tokens_wide * tokens_wide, axis=-1, keepdims=True)
    normed = (tokens_wide * lax.rsqrt(mean_square + 1e-06)).astype(jnp.bfloat16)
    out_grad = (cotangent[0].astype(jnp.float32) * live_mask[:, None] / live_count).astype(
        jnp.bfloat16
    )
    up_whole, down_whole = (
        lax.all_gather(up_half, "dp", axis=2, tiled=True),
        lax.all_gather(down_half, "dp", axis=2, tiled=True),
    )
    pre_act = jnp.dot(normed, up_whole[0], preferred_element_type=jnp.float32) * up_scale
    gate_sig = jax.nn.sigmoid(pre_act)
    act_out = (pre_act * gate_sig).astype(jnp.bfloat16)
    act_grad = (
        lax.dot_general(
            out_grad, down_whole[0], (((1,), (1,)), ((), ())), preferred_element_type=jnp.float32
        )
        * down_scale
    )
    pre_grad = (act_grad * gate_sig * (1.0 + pre_act * (1.0 - gate_sig))).astype(jnp.bfloat16)
    up_term = up_scale * jnp.einsum(
        "td,tf->df", normed, pre_grad, preferred_element_type=jnp.float32
    )
    down_term = down_scale * jnp.einsum(
        "tf,td->fd", act_out, out_grad, preferred_element_type=jnp.float32
    )
    up_grad, down_grad = (
        lax.psum_scatter(
            up_term.astype(jnp.bfloat16), "dp", scatter_dimension=1, tiled=True
        ).astype(jnp.float32),
        lax.psum_scatter(
            down_term.astype(jnp.bfloat16), "dp", scatter_dimension=1, tiled=True
        ).astype(jnp.float32),
    )
    up_delta = inner_update(up_half[0], up_grad, up_first[0], up_second[0])
    down_delta = inner_update(down_half[0], down_grad, down_first[0], down_second[0])
    up_rows = up_master.shape[1]
    up_cols = up_delta.shape[1]
    down_rows = down_master.shape[1]
    down_cols = down_delta.shape[1]
    up_sent = up_delta.reshape(path_count, up_rows, up_cols)
    down_sent = down_delta.reshape(path_count, up_rows, up_cols)
    levels = jnp.arange(C, dtype=jnp.int32)
    up_onehot = up_choice[None, :] == levels[:, None]
    down_onehot = down_choice[None, :] == levels[:, None]
    up_sum = jnp.einsum(
        "cp,prx->crx",
        up_onehot.astype(jnp.bfloat16),
        lax.all_to_all(up_sent, "path", split_axis=0, concat_axis=0, tiled=True),
        preferred_element_type=jnp.float32,
    )
    down_sum = jnp.einsum(
        "cp,prx->crx",
        down_onehot.astype(jnp.bfloat16),
        lax.all_to_all(down_sent, "path", split_axis=0, concat_axis=0, tiled=True),
        preferred_element_type=jnp.float32,
    )
    down_total = down_sum.reshape(down_sum.shape[0], down_rows, down_cols)
    up_used = jnp.sum(up_onehot.astype(jnp.float32), axis=1)
    down_used = jnp.sum(down_onehot.astype(jnp.float32), axis=1)
    up_mean = up_sum / jnp.maximum(up_used, 1.0)[:, None, None]
    down_mean = down_total / jnp.maximum(down_used, 1.0)[:, None, None]
    new_up_momentum = 0.9 * up_momentum + up_mean
    new_down_momentum = 0.9 * down_momentum + down_mean
    new_up_master = up_master - 0.7 * (up_mean + 0.9 * new_up_momentum)
    new_down_master = down_master - 0.7 * (down_mean + 0.9 * new_down_momentum)
    return (new_up_master, new_down_master, new_up_momentum, new_down_momentum)


def solution(mesh):
    placed = (
        P("path", "dp", None),
        P("path", "dp", None),
        P("path", "dp"),
        P(),
        P(None, "path", "dp"),
        P(None, "path", "dp"),
        P(None, "path", "dp"),
        P(None, "path", "dp"),
        P("path", None, "dp"),
        P("path", None, "dp"),
        P("path", None, "dp"),
        P("path", None, "dp"),
    )
    return jax.shard_map(
        shards,
        mesh=mesh,
        in_specs=placed,
        out_specs=(
            P(None, "path", "dp"),
            P(None, "path", "dp"),
            P(None, "path", "dp"),
            P(None, "path", "dp"),
        ),
        check_vma=False,
    )
```

profile of v0, /device:TPU:6, one launch (start us, length us, event | category | flops | bytes accessed | tf_op | source)
XLA Modules:
  0.0 704.8 jit_solution(848958796616845127)
XLA Ops:
  7.2 0.0 all-gather.5.cloned.1.call-start
  7.2 0.8 slice_bitcast_fusion
  8.0 0.8 and_bitcast_fusion.1
  8.7 1.3 convert_element_type.119
  10.0 2.8 gather_fusion.1
  12.8 2.6 broadcast_select_fusion
  15.4 0.0 copy-start
  15.4 59.3 %all_to_all.34 = bf16[64,16,2048]{2,1,0:T(8,128)(2,1)} all-to-all(bf16[64,16,2048]{2,1,0:T(8,128)(2,1)S(1)} %broadcast_select_fusion), channel_id=1, replica_groups=mesh['path'=64,'dp'=2] {'path'}, dimensions={0} | all-to-all | bytes 8388608 | tf_op jit(solution)/shard_map/all_to_all | solution.py:42
  74.7 0.0 all-gather.5.cloned.1.call-update
  74.8 0.0 all-gather.3.cloned.1.call-start
  74.8 0.1 convert_element_type.115
  74.9 2.8 gather_fusion
  77.7 2.6 broadcast_select_fusion.1
  80.3 0.0 copy-start.2
  80.3 65.7 %all_to_all.35 = bf16[64,64,512]{2,1,0:T(8,128)(2,1)} all-to-all(bf16[64,64,512]{2,1,0:T(8,128)(2,1)S(1)} %broadcast_select_fusion.1), channel_id=1, replica_groups=mesh['path'=64,'dp'=2] {'path'}, dimensions={0} | all-to-all | bytes 8388608 | tf_op jit(solution)/shard_map/all_to_all | solution.py:43
  146.0 0.0 all-gather.3.cloned.1.call-update
  146.1 0.0 reduce-scatter.3.cloned.1.call-start
  146.1 0.6 fusion.63
  146.7 7.1 %psum.7 = f32[]{:T(128)} all-reduce(f32[]{:T(128)} %get-tuple-element.17), channel_id=1, replica_groups=mesh['path'=64,'dp'=2] {'dp'}, use_global_device_ids=true, to_apply=%region_2.3 | all-reduce | flops 1 | bytes 8 | tf_op jit(solution)/shard_map/psum | solution.py:46
  153.8 0.2 fusion.40
  154.1 73.6 %all-gather.5.cloned.1.call-done = bf16[1,1024,4096]{2,1,0:T(8,128)(2,1)} async-done(((bf16[1,1024,2048]{2,1,0:T(8,128)(2,1)}), bf16[1,1024,4096]{2,1,0:T(8,128)(2,1)}) %all-gather.5.cloned.1.call-update) | async-done | bytes 8388624 | tf_op jit(solution)/shard_map/all_gather | solution.py:54
  227.6 8.8 %fusion.22 = f32[384,4096]{1,0:T(8,128)} fusion(bf16[1,1024,4096]{2,1,0:T(8,128)(2,1)} %all-gather.5.cloned.1.call-done, bf16[1,384,1024]{2,1,0:T(8,128)(2,1)S(1)} %copy-done.2, f32[384]{0:T(512)S(1)} %add_rsqrt_fusion), kind=kOutput, calls=%fused_computation.33 | convolution fusion | flops 3223977984 | bytes 15468032 | tf_op jit(solution)/shard_map/dot_general | solution.py:57
  236.5 100.2 %all-gather.3.cloned.1.call-done = bf16[1,4096,1024]{2,1,0:T(8,128)(2,1)} async-done(((bf16[1,4096,512]{2,1,0:T(8,128)(2,1)}), bf16[1,4096,1024]{2,1,0:T(8,128)(2,1)}) %all-gather.3.cloned.1.call-update) | async-done | bytes 8388624 | tf_op jit(solution)/shard_map/all_gather | solution.py:55
  336.6 11.7 %multiply_convert_fusion.3 = bf16[384,4096]{1,0:T(8,128)(2,1)S(1)} fusion(f32[384,4096]{1,0:T(8,128)} %fusion.22, bf16[1,4096,1024]{2,1,0:T(8,128)(2,1)} %all-gather.3.cloned.1.call-done, bf16[1,384,1024]{2,1,0:T(8,128)(2,1)S(1)} %copy-done.4, f32[]{:T(128)} %psum.7, f32[384]{0:T(512)S(1)} %get-tuple-element.16), kind=kOutput, calls=%fused_computation.31 | convolution fusion | flops 3238526976 | bytes 18613764 | tf_op jit(solution)/shard_map/dot_general | solution.py:61
  348.4 6.9 multiply_convert_fusion.1
  355.3 0.0 reduce-scatter.3.cloned.1.call-update
  355.3 0.2 reduce-scatter.5.cloned.1.call-start
  355.6 11.2 %multiply_convert_fusion = bf16[4096,1024]{1,0:T(8,128)(2,1)} fusion(f32[384,4096]{1,0:T(8,128)} %fusion.22, bf16[1,384,1024]{2,1,0:T(8,128)(2,1)S(1)} %copy-done.4, f32[]{:T(128)} %psum.7, f32[384]{0:T(512)S(1)} %get-tuple-element.16), kind=kOutput, calls=%fused_computation.2 | convolution fusion | flops 3239051264 | bytes 15468036 | tf_op jit(solution)/shard_map/tf,td->fd/dot_general | solution.py:70
  366.8 0.0 reduce-scatter.5.cloned.1.call-update
  366.8 6.6 convert_multiply_fusion.3
  373.4 84.8 %reduce-scatter.3.cloned.1.call-done = bf16[1024,2048]{1,0:T(8,128)(2,1)} async-done(((bf16[1024,4096]{1,0:T(8,128)(2,1)}), bf16[1024,2048]{1,0:T(8,128)(2,1)}) %reduce-scatter.3.cloned.1.call-update) | async-done | bytes 4194320 | tf_op jit(solution)/shard_map/reduce_scatter | solution.py:74
  458.2 11.5 %fusion.19 = bf16[1024,2048]{1,0:T(8,128)(2,1)} fusion(f32[64,16,2048]{2,1,0:T(8,128)} %convert_multiply_fusion.3, bf16[1,1024,2048]{2,1,0:T(8,128)(2,1)} %param.21, bf16[1024,2048]{1,0:T(8,128)(2,1)} %reduce-scatter.3.cloned.1.call-done, bf16[1,1024,2048]{2,1,0:T(8,128)(2,1)} %param.20), kind=kLoop, calls=%fused_computation.29 | loop fusion | flops 31457280 | bytes 25165824 | tf_op jit(solution)/shard_map/convert_element_type | solution.py:15
  469.7 8.4 %all-to-all-start.2 = ((bf16[64,16,2048]{2,1,0:T(8,128)(2,1)}), bf16[64,16,2048]{2,1,0:T(8,128)(2,1)}, u32[]{:S(2)}, u32[]{:S(2)}) async-start(bf16[64,16,2048]{2,1,0:T(8,128)(2,1)} %bitcast.86), calls=%async_computation.3 | async-start | bytes 8388608 | tf_op jit(solution)/shard_map/all_to_all | solution.py:95
  478.1 6.9 convert_multiply_fusion.2
  485.0 123.4 %reduce-scatter.5.cloned.1.call-done = bf16[4096,512]{1,0:T(8,128)(2,1)} async-done(((bf16[4096,1024]{1,0:T(8,128)(2,1)}), bf16[4096,512]{1,0:T(8,128)(2,1)}) %reduce-scatter.5.cloned.1.call-update) | async-done | bytes 4194320 | tf_op jit(solution)/shard_map/reduce_scatter | solution.py:77
  608.4 11.5 %fusion.18 = bf16[4096,512]{1,0:T(8,128)(2,1)} fusion(f32[64,64,512]{2,1,0:T(8,128)} %convert_multiply_fusion.2, bf16[1,4096,512]{2,1,0:T(8,128)(2,1)} %param.23, bf16[4096,512]{1,0:T(8,128)(2,1)} %reduce-scatter.5.cloned.1.call-done, bf16[1,4096,512]{2,1,0:T(8,128)(2,1)} %param.22), kind=kLoop, calls=%fused_computation.28 | loop fusion | flops 31457280 | bytes 25165824 | tf_op jit(solution)/shard_map/convert_element_type | solution.py:15
  619.8 7.6 %reshape.97 = bf16[64,16,2048]{2,1,0:T(8,128)(2,1)} reshape(bf16[4096,512]{1,0:T(8,128)(2,1)} %fusion.18) | data formatting | bytes 8388608 | tf_op jit(solution)/shard_map/reshape | solution.py:88
  627.4 10.0 %all-to-all-start.3 = ((bf16[64,16,2048]{2,1,0:T(8,128)(2,1)}), bf16[64,16,2048]{2,1,0:T(8,128)(2,1)}, u32[]{:S(2)}, u32[]{:S(2)}) async-start(bf16[64,16,2048]{2,1,0:T(8,128)(2,1)} %reshape.97), calls=%async_computation.5 | async-start | bytes 8388608 | tf_op jit(solution)/shard_map/all_to_all | solution.py:101
  637.4 0.1 convert_reduce_fusion.1
  637.5 0.1 convert_reduce_fusion
  637.7 8.2 %fusion.43 = (f32[8,16,2048]{2,0,1:T(8,128)S(1)}, f32[8,16,2048]{2,0,1:T(8,128)S(1)}) fusion(f32[8,16,2048]{2,1,0:T(8,128)} %param.18, f32[8,16,2048]{2,1,0:T(8,128)S(1)} %copy-done.1, f32[8]{0:T(128)S(1)} %broadcast_maximum_fusion.1, bf16[64,16,2048]{2,1,0:T(8,128)(2,1)} %all-to-all-done.2, s32[64]{0:T(128)S(1)} %get-tuple-element.25), kind=kOutput, calls=%fused_computation.58 | convolution fusion | flops 35389952 | bytes 8388896 | tf_op jit(solution)/shard_map/cp,prx->crx/dot_general | solution.py:92
  645.9 1.6 copy.34
  647.5 1.6 copy.35
  649.0 38.3 %all-to-all-done.3 = bf16[64,16,2048]{2,1,0:T(8,128)(2,1)} async-done(((bf16[64,16,2048]{2,1,0:T(8,128)(2,1)}), bf16[64,16,2048]{2,1,0:T(8,128)(2,1)}, u32[]{:S(2)}, u32[]{:S(2)}) %all-to-all-start.3) | async-done | bytes 4194336 | tf_op jit(solution)/shard_map/all_to_all | solution.py:101
  687.3 6.7 fusion.25
  694.0 0.6 copy.33
  694.6 0.3 reshape.98
  694.9 3.0 multiply_subtract_fusion
  (13 shorter events, 0.0 us)
Async XLA Ops:
  7.2 220.5 %all-gather.5.cloned.1.call-start = ((), (), s32[]{:S(2)}) async-start(), calls=%async_computation.7 | async-start | bytes 12582912 | tf_op jit(solution)/shard_map/all_gather | solution.py:54
  15.4 59.4 %copy-start = (f32[8,64,512]{2,1,0:T(8,128)S(1)}, f32[8,64,512]{2,1,0:T(8,128)}, u32[]{:S(2)}) copy-start(f32[8,64,512]{2,1,0:T(8,128)} %param.17) | copy-start | bytes 3145732
  74.8 261.9 %all-gather.3.cloned.1.call-start = ((), (), s32[]{:S(2)}) async-start(), calls=%async_computation.6 | async-start | bytes 12582912 | tf_op jit(solution)/shard_map/all_gather | solution.py:55
  80.3 65.8 %copy-start.3 = (s32[1,384]{1,0:T(1,128)S(1)}, s32[1,384]{1,0:T(1,128)}, u32[]{:S(2)}) copy-start(s32[1,384]{1,0:T(1,128)} %param.14) | copy-start | bytes 4612
  80.3 73.5 %copy-start.2 = (bf16[1,384,1024]{2,1,0:T(8,128)(2,1)S(1)}, bf16[1,384,1024]{2,1,0:T(8,128)(2,1)}, u32[]{:S(2)}) copy-start(bf16[1,384,1024]{2,1,0:T(8,128)(2,1)} %param.12) | copy-start | bytes 2359300
  146.1 312.1 %reduce-scatter.3.cloned.1.call-start = ((), (), s32[]{:S(2)}) async-start(), calls=%async_computation.8 | async-start | bytes 12582912 | tf_op jit(solution)/shard_map/reduce_scatter | solution.py:74
  154.1 182.6 %copy-start.4 = (bf16[1,384,1024]{2,1,0:T(8,128)(2,1)S(1)}, bf16[1,384,1024]{2,1,0:T(8,128)(2,1)}, u32[]{:S(2)}) copy-start(bf16[1,384,1024]{2,1,0:T(8,128)(2,1)} %param.13) | copy-start | bytes 2359300
  355.3 253.1 %reduce-scatter.5.cloned.1.call-start = ((), (), s32[]{:S(2)}) async-start(), calls=%async_computation.9 | async-start | bytes 12582912 | tf_op jit(solution)/shard_map/reduce_scatter | solution.py:77
  469.7 157.7 %all-to-all-start.2 = ((bf16[64,16,2048]{2,1,0:T(8,128)(2,1)}), bf16[64,16,2048]{2,1,0:T(8,128)(2,1)}, u32[]{:S(2)}, u32[]{:S(2)}) async-start(bf16[64,16,2048]{2,1,0:T(8,128)(2,1)} %bitcast.86), calls=%async_computation.3 | async-start | bytes 8388608 | tf_op jit(solution)/shard_map/all_to_all | solution.py:95
  627.4 10.3 %copy-start.1 = (f32[8,16,2048]{2,1,0:T(8,128)S(1)}, f32[8,16,2048]{2,1,0:T(8,128)}, u32[]{:S(2)}) copy-start(f32[8,16,2048]{2,1,0:T(8,128)} %param.16) | copy-start | bytes 3145732
  627.4 59.9 %all-to-all-start.3 = ((bf16[64,16,2048]{2,1,0:T(8,128)(2,1)}), bf16[64,16,2048]{2,1,0:T(8,128)(2,1)}, u32[]{:S(2)}, u32[]{:S(2)}) async-start(bf16[64,16,2048]{2,1,0:T(8,128)(2,1)} %reshape.97), calls=%async_computation.5 | async-start | bytes 8388608 | tf_op jit(solution)/shard_map/all_to_all | solution.py:101
Sparse Core Ops, SparseCore 0:
  74.9 152.7 all-gather.4
  229.3 107.3 all-gather.2
  355.5 102.7 reduce-scatter.2
  460.6 147.7 reduce-scatter.4
where the time goes:
time: 716 us; the launch traced here: 705 us
  waiting for transfers between devices  420 us (59%)
  blocking collectives  132 us (18%)
  matrix products  53.6 us (7%)
  other arithmetic  48.7 us (7%)
  starting transfers between devices  18.7 us (3%)
  local copies, waits for them, and re-layouts  17.2 us (2%)
  between operations  14.3 us (2%)
    reduce_scatter x1, waiting for transfers between devices, shards(): lax.psum_scatter(down_term.astype(jnp.bfloat16), 'dp', scatter_dimension=...  123 us
    all_gather x1, waiting for transfers between devices, shards(): lax.all_gather(down_half, 'dp', axis=2, tiled=True)  100 us
    reduce_scatter x1, waiting for transfers between devices, shards(): lax.psum_scatter(up_term.astype(jnp.bfloat16), 'dp', scatter_dimension=1,...  84.8 us
    all_gather x1, waiting for transfers between devices, shards(): lax.all_gather(up_half, 'dp', axis=2, tiled=True)  73.6 us
    all_to_all x1, blocking collectives, shards(): lax.all_to_all(down_pick, 'path', split_axis=0, concat_axis=1, tiled=True)  65.7 us
    all_to_all x1, blocking collectives, shards(): lax.all_to_all(up_pick, 'path', split_axis=0, concat_axis=1, tiled=True)  59.3 us
    all_to_all x1, waiting for transfers between devices, shards(): lax.all_to_all(down_sent, 'path', split_axis=0, concat_axis=0, tiled=True)  38.3 us
    convert_element_type x2, other arithmetic, inner_update(): return (0.1 * direction).astype(jnp.bfloat16)  23 us
  transfers between devices with their start and end apart: 6, of which 5 were waited for; matrix products, arithmetic and copies ran while one was open for 12% of the time, Pallas kernels for 0%

commit v1 on v0

v1 whole, which is shorter than its diff:
```python
import jax
import jax.numpy as jnp
from jax import lax
from jax.experimental import pallas as pl
from jax.experimental.pallas import tpu as pltpu
from jax.sharding import PartitionSpec as P

D = 1024
F = 4096
C = 8
TOK = 384
HALF_F = F // 2
HALF_D = D // 2
GROUP = 32
MESH = pl.DeviceIdType.MESH
BF16 = jnp.bfloat16
F32 = jnp.float32
NT = (((1,), (1,)), ((), ()))
TN = (((0,), (0,)), ((), ()))
UP_SCALE = D ** (-0.5)
DOWN_SCALE = F ** (-0.5)


def step_direction(gradient, first_moment, second_moment):
    first_new = 0.9 * first_moment.astype(F32) + 0.1 * gradient
    second_new = 0.95 * second_moment.astype(F32) + 0.05 * gradient * gradient
    return (0.1 * first_new / (jnp.sqrt(second_new) + 1e-08)).astype(BF16)


def kernel(
    table, coef, choice, live, act_in, cot_in, um_in, dm_in, umom_in, dmom_in, up_first, up_second,
    down_first, down_second, um_out, dm_out, umom_out, dmom_out,
    um, dm, umom, dmom, act, cot, upb, upf, dnb, blk, buf_a, buf_b, wup, wdn, rdn, rup,
    gsend, gmine, grecv, nrm, og, count, gp, mom, pdn_send, pdn_recv, pup_send, pup_recv, pick_up, pick_dn,
    in_sem, mom_sem, out_sem, y_send, y_recv, dn_send, blk_recv, wu_send, wu_recv, wd_send, wd_recv,
    g_send, g_recv, dd_send, dd_recv, du_send, du_recv,
):
    path = lax.axis_index("path")
    here = lax.axis_index("dp")
    x = lax.div(path, 16)
    yl = lax.rem(lax.div(path, 8), 2)
    zc = lax.rem(path, 8)
    z = lax.div(zc, 2)
    core = lax.rem(zc, 2)
    group = x * 8 + zc
    other_yl = 1 - yl
    there = 1 - here

    def place(x_, yl_, zc_):
        return x_ * 16 + yl_ * 8 + zc_

    def zc_at(k):
        return lax.rem(z + lax.rem(lax.div(k, 2), 4), 4) * 2 + lax.rem(core + k, 2)

    def peer(k):
        return lax.rem(x + lax.div(k, 8), 4), zc_at(k)

    def remote(src, dst, send, recv, to_path, to_dp):
        return pltpu.make_async_remote_copy(
            src_ref=src, dst_ref=dst, send_sem=send, recv_sem=recv,
            device_id=(to_path, to_dp), device_id_type=MESH,
        )

    def settle(ref, sem):
        pltpu.make_async_copy(ref, ref, sem).wait()

    loads = [
        pltpu.make_async_copy(src, dst, in_sem.at[i])
        for i, (src, dst) in enumerate(
            [(um_in, um), (act_in, act), (dm_in, dm), (cot_in, cot), (umom_in, umom), (dmom_in, dmom)]
        )
    ]
    for load in loads:
        load.start()

    cross = lax.rem(lax.div(x, 2) + here, 2)
    barrier = pltpu.get_barrier_semaphore()

    def greet(k, _):
        x_, zc_ = peer(k)
        pl.semaphore_signal(barrier, inc=1, device_id=(place(x_, yl, zc_), here), device_id_type=MESH)
        return 0

    lax.fori_loop(1, GROUP, greet, 0)
    for to_path, to_dp in (
        (place(x, other_yl, zc), here),
        (path, there),
        (place(3 - x, yl, zc), there),
        (place(3 - x, other_yl, zc), there),
    ):
        pl.semaphore_signal(barrier, inc=1, device_id=(to_path, to_dp), device_id_type=MESH)

    def pick_up_rows(side, source):
        def one(k, _):
            module = table[2 * (lax.div(k, 8) * 16 + yl * 8 + lax.rem(k, 8))]
            buf_a[side * GROUP + k] = source[module]
            return 0

        lax.fori_loop(0, GROUP, one, 0)

    loads[0].wait()
    upb[...] = um[...].astype(BF16)
    pick_up_rows(yl, upb)
    pl.semaphore_wait(barrier, GROUP + 3)

    up_swap = remote(upb, upf, y_send.at[0], y_recv.at[0], place(x, other_yl, zc), here)
    up_swap.start()

    def send_up_rows(side):
        row = place(x, side, zc)
        pltpu.make_async_copy(buf_a.at[side * GROUP + group], wup.at[row], wu_recv).start()

        def one(k, _):
            x_, zc_ = peer(lax.rem(k * 11, GROUP))
            remote(
                buf_a.at[side * GROUP + x_ * 8 + zc_], wup.at[row], wu_send, wu_recv, place(x_, yl, zc_), here
            ).start()
            return 0

        lax.fori_loop(1, GROUP, one, 0)

    send_up_rows(yl)

    own_rows = pl.ds(pl.multiple_of(here * TOK, TOK), TOK)
    loads[1].wait()
    for part in range(3):
        rows = pl.ds(part * 128, 128)
        wide = act[rows, :].astype(F32)
        mean_square = jnp.mean(wide * wide, axis=-1, keepdims=True)
        to_rows = pl.ds(pl.multiple_of(here * TOK + part * 128, 128), 128)
        nrm[to_rows, :] = (wide * lax.rsqrt(mean_square + 1e-06)).astype(BF16)
    nrm_swap = remote(nrm.at[own_rows], nrm.at[own_rows], y_send.at[1], y_recv.at[1], path, there)
    nrm_swap.start()

    loads[2].wait()
    dnb[...] = dm[...].astype(BF16)
    x_to = x + cross * (3 - 2 * x)
    dp_to = here + cross * (1 - 2 * here)
    dn_far = remote(dnb, blk.at[yl], dn_send.at[0], blk_recv, place(x_to, other_yl, zc), dp_to)
    dn_far.start()
    dn_near = remote(dnb, blk.at[yl], dn_send.at[1], blk_recv, place(3 - x, yl, zc), there)

    @pl.when(cross == 1)
    def _():
        dn_near.start()

    @pl.when(cross == 0)
    def _():
        pltpu.make_async_copy(dnb, blk.at[yl], blk_recv).start()

    loads[3].wait()
    for part in range(3):
        rows = pl.ds(part * 128, 128)
        to_rows = pl.ds(pl.multiple_of(here * TOK + part * 128, 128), 128)
        og[to_rows, :] = (cot[rows, :].astype(F32) * live[rows, :]).astype(BF16)
    count[0] = jnp.broadcast_to(jnp.sum(live[...]), (8, 128))
    og_swap = remote(og.at[own_rows], og.at[own_rows], y_send.at[2], y_recv.at[2], path, there)
    og_swap.start()
    count_swap = remote(count.at[0], count.at[1], y_send.at[3], y_recv.at[3], path, there)
    count_swap.start()

    up_swap.wait()
    pick_up_rows(other_yl, upf)
    send_up_rows(other_yl)

    settle(blk, blk_recv)

    def pick_down_rows(k, _):
        module = table[2 * (lax.div(k, 8) * 16 + yl * 8 + lax.rem(k, 8)) + 1]
        buf_b[k] = blk[0, module]
        buf_b[GROUP + k] = blk[1, module]
        return 0

    lax.fori_loop(0, GROUP, pick_down_rows, 0)

    nrm_swap.wait()
    og_swap.wait()
    count_swap.wait()
    per_count = 1.0 / (count[0] + count[1])
    per_count = per_count[0:1, 0:1]

    def scale_rows(i, _):
        rows = pl.ds(pl.multiple_of(i * 64, 64), 64)
        og[rows, :] = (og[rows, :].astype(F32) * per_count).astype(BF16)
        return 0

    lax.fori_loop(0, 12, scale_rows, 0)

    settle(buf_a.at[pl.ds(0, 2 * GROUP - 2)], wu_send)
    from_x = x_to - 2 * here
    for side in range(2):
        row = from_x * 16 + side * 8 + zc
        pltpu.make_async_copy(buf_b.at[side * GROUP + group], wdn.at[dp_to, row], wd_recv).start()

        def one(k, _, side=side, row=row):
            x_, zc_ = peer(lax.rem(k * 11, GROUP))
            remote(
                buf_b.at[side * GROUP + x_ * 8 + zc_], wdn.at[dp_to, row], wd_send, wd_recv,
                place(x_, yl, zc_), here,
            ).start()
            return 0

        lax.fori_loop(1, GROUP, one, 0)

    down_x = [here * 2 + lax.rem(x + i, 2) for i in range(2)] + [there * 2 + lax.rem(x + i, 2) for i in range(2)]
    up_x = [lax.rem(x + i, 4) for i in (2, 1, 3, 0)]

    def fetch(step):
        slot = step % 2
        for kind, (down_source, up_source) in enumerate(((down_first, up_first), (down_second, up_second))):
            if step < 4:
                rows = pl.ds(pl.multiple_of(down_x[step] * 1024, 1024), 1024)
                pltpu.make_async_copy(
                    down_source.at[rows], mom.at[slot, kind], mom_sem.at[slot, kind]
                ).start()
            else:
                rows = pl.ds(pl.multiple_of(up_x[step - 4] * 256, 256), 256)
                for b in range(4):
                    pltpu.make_async_copy(
                        up_source.at[rows, pl.ds(b * 512, 512)],
                        mom.at[slot, kind, pl.ds(b * 256, 256)],
                        mom_sem.at[slot, kind],
                    ).start()

    def await_moments(step):
        slot = step % 2
        for kind in range(2):
            settle(mom.at[slot, kind], mom_sem.at[slot, kind])

    fetch(0)
    fetch(1)

    settle(wup, wu_recv)
    mine_cols = pl.ds(pl.multiple_of(here * HALF_D, HALF_D), HALF_D)
    their_cols = pl.ds(pl.multiple_of(there * HALF_D, HALF_D), HALF_D)

    def g_copy(chunk):
        rows = pl.ds(pl.multiple_of(chunk * 512, 512), 512)
        return remote(gsend.at[rows], grecv.at[rows], g_send.at[chunk], g_recv.at[chunk], path, there)

    def hidden(i, _):
        cols = pl.ds(pl.multiple_of(i * 256, 256), 256)
        weights = wup[:, :, cols].reshape(D, 256)
        pre = jnp.dot(nrm[...], weights, preferred_element_type=F32) * UP_SCALE
        sig = 0.5 * jnp.tanh(0.5 * pre) + 0.5
        out = (pre * sig).astype(BF16)
        gp[:, cols] = (sig * (1.0 + pre * (1.0 - sig))).astype(BF16)
        theirs = lax.dot_general(out, og[:, their_cols], TN, preferred_element_type=F32)
        gsend[cols, :] = (theirs * DOWN_SCALE).astype(BF16)

        @pl.when(lax.rem(i, 2) == 1)
        def _():
            g_copy(lax.div(i, 2)).start()

        mine = lax.dot_general(out, og[:, mine_cols], TN, preferred_element_type=F32)
        gmine[cols, :] = (mine * DOWN_SCALE).astype(BF16)
        return 0

    lax.fori_loop(0, 8, hidden, 0)

    def down_step(step):
        x_ = down_x[step]
        source = gmine if step < 2 else grecv
        first_row = lax.rem(x_, 2) * 1024
        if step >= 2:
            for half in range(2):
                g_copy(lax.rem(x_, 2) * 2 + half).wait_recv()
        await_moments(step)
        slot = step % 2

        def one(q, _):
            rows = pl.ds(pl.multiple_of(q * 64, 64), 64)
            grad = source[pl.ds(pl.multiple_of(first_row + q * 64, 64), 64), :].astype(F32)
            delta = step_direction(grad, mom[slot, 0, rows, :], mom[slot, 1, rows, :])
            for b in range(4):
                buf_a[x_ * 16 + q, :, pl.ds(b * 512, 512)] = delta[b * 16 : b * 16 + 16, :]
            return 0

        lax.fori_loop(0, 16, one, 0)
        fetch(step + 2)

        def send(k, _):
            zc_ = zc_at(lax.rem(k, 8))
            side = lax.rem(other_yl + lax.div(k, 8), 2)
            row = x_ * 16 + side * 8 + zc_
            away = (x_ * 8 + zc_) != group

            @pl.when(away)
            def _():
                remote(
                    buf_a.at[row], rdn.at[side, group], dd_send, dd_recv.at[side], place(x_, yl, zc_), here
                ).start()

            @pl.when(jnp.logical_not(away))
            def _():
                pltpu.make_async_copy(buf_a.at[row], rdn.at[side, group], dd_recv.at[side]).start()

            return 0

        lax.fori_loop(0, 16, send, 0)

    down_step(0)
    down_step(1)

    settle(wdn, wd_recv)

    def hidden_grad(i, _):
        cols = pl.ds(pl.multiple_of(i * 256, 256), 256)
        low = wdn[0, pl.ds(i * 4, 4)].reshape(256, HALF_D)
        high = wdn[1, pl.ds(i * 4, 4)].reshape(256, HALF_D)
        grad = lax.dot_general(og[:, pl.ds(0, HALF_D)], low, NT, preferred_element_type=F32)
        grad += lax.dot_general(og[:, pl.ds(HALF_D, HALF_D)], high, NT, preferred_element_type=F32)
        gp[:, cols] = (grad * DOWN_SCALE * gp[:, cols].astype(F32)).astype(BF16)
        return 0

    lax.fori_loop(0, 8, hidden_grad, 0)
    settle(buf_b.at[pl.ds(0, 2 * GROUP - 2)], wd_send)
    down_step(2)
    down_step(3)

    def send_up_delta(x_, zc_, side):
        row = x_ * 16 + side * 8 + zc_
        away = (x_ * 8 + zc_) != group

        @pl.when(away)
        def _():
            remote(
                buf_b.at[row], rup.at[side, group], du_send, du_recv.at[side], place(x_, yl, zc_), here
            ).start()

        @pl.when(jnp.logical_not(away))
        def _():
            pltpu.make_async_copy(buf_b.at[row], rup.at[side, group], du_recv.at[side]).start()

    def up_step(step):
        x_ = up_x[step - 4]
        await_moments(step)
        slot = step % 2
        lhs = nrm[:, pl.ds(pl.multiple_of(x_ * 256, 256), 256)]

        def one(b, _):
            cols = pl.ds(pl.multiple_of(b * 512, 512), 512)
            rows = pl.ds(pl.multiple_of(b * 256, 256), 256)
            grad = lax.dot_general(lhs, gp[:, cols], TN, preferred_element_type=F32) * UP_SCALE
            delta = step_direction(grad, mom[slot, 0, rows, :], mom[slot, 1, rows, :])
            buf_b[pl.ds(x_ * 16, 16), pl.ds(pl.multiple_of(b * 16, 16), 16), :] = delta.reshape(16, 16, 512)
            return 0

        lax.fori_loop(0, 4, one, 0)
        if step + 2 < 8:
            fetch(step + 2)

        def send(k, _):
            send_up_delta(x_, zc_at(k), other_yl)
            return 0

        lax.fori_loop(0, 8, send, 0)

    for step in range(4, 8):
        up_step(step)

    def send_rest(k, _):
        x_, zc_ = peer(lax.rem(k * 11, GROUP))
        send_up_delta(x_, zc_, yl)
        return 0

    lax.fori_loop(0, GROUP, send_rest, 0)

    module_row = lax.broadcasted_iota(jnp.int32, (C * 16, GROUP * 16), 0)
    path_row = lax.broadcasted_iota(jnp.int32, (C * 16, GROUP * 16), 1)
    same_row = (module_row & 15) == (path_row & 15)
    module = module_row >> 4
    pick_up[...] = jnp.where(same_row & (module == choice[0:1, :]), 1.0, 0.0).astype(BF16)
    pick_dn[...] = jnp.where(same_row & (module == choice[1:2, :]), 1.0, 0.0).astype(BF16)

    def down_sum(side, b):
        block = rdn[side, :, :, pl.ds(b * 512, 512)].reshape(GROUP * 16, 512)
        return jnp.dot(pick_dn[...], block, preferred_element_type=F32).reshape(C, 16, 512)

    def up_sum(side, b):
        block = rup[side, :, pl.ds(b * 16, 16), :].reshape(GROUP * 16, 512)
        return jnp.dot(pick_up[...], block, preferred_element_type=F32).reshape(C, 16, 512)

    def finish(total, master, momentum, level, rows, cols):
        for m in range(C):
            weights = master[m, rows, cols]
            mean = total[m] * coef[level * 16 + m] + coef[level * 16 + 8 + m] * weights.astype(BF16).astype(F32)
            speed = 0.9 * momentum[m, rows, cols] + mean
            momentum[m, rows, cols] = speed
            master[m, rows, cols] = weights - 0.7 * (mean + 0.9 * speed)

    mate = place(x, other_yl, zc)
    settle(rdn.at[other_yl], dd_recv.at[other_yl])
    for b in range(4):
        pdn_send[:, :, pl.ds(b * 512, 512)] = down_sum(other_yl, b).astype(BF16)
    dn_part = remote(pdn_send, pdn_recv, y_send.at[4], y_recv.at[4], mate, here)
    dn_part.start()
    settle(rdn.at[yl], dd_recv.at[yl])
    for load in loads[4:]:
        load.wait()
    dn_part.wait()
    for b in range(4):
        cols = pl.ds(b * 512, 512)
        total = down_sum(yl, b) + pdn_recv[:, :, cols].astype(F32)
        finish(total, dm, dmom, 1, pl.ds(b * 16, 16), pl.ds(0, 512))
    stores = [
        pltpu.make_async_copy(src, dst, out_sem.at[i])
        for i, (src, dst) in enumerate([(dm, dm_out), (dmom, dmom_out), (um, um_out), (umom, umom_out)])
    ]
    stores[0].start()
    stores[1].start()

    settle(rup.at[other_yl], du_recv.at[other_yl])
    for b in range(4):
        pup_send[:, pl.ds(b * 16, 16), :] = up_sum(other_yl, b).astype(BF16)
    up_part = remote(pup_send, pup_recv, y_send.at[5], y_recv.at[5], mate, here)
    up_part.start()
    settle(rup.at[yl], du_recv.at[yl])
    up_part.wait()
    for b in range(4):
        rows = pl.ds(b * 16, 16)
        total = up_sum(yl, b) + pup_recv[:, rows, :].astype(F32)
        finish(total, um, umom, 0, pl.ds(0, 16), pl.ds(b * 512, 512))
    stores[2].start()
    stores[3].start()

    dn_far.wait_send()

    @pl.when(cross == 1)
    def _():
        dn_near.wait_send()

    for chunk in range(4):
        g_copy(chunk).wait_send()
    settle(buf_a.at[pl.ds(0, 2 * GROUP - 2)], dd_send)
    settle(buf_b.at[pl.ds(0, 2 * GROUP - 2)], du_send)
    for store in stores:
        store.wait()


def shards(
    activations,
    cotangent,
    token_ids,
    path_table,
    up_master,
    down_master,
    up_momentum,
    down_momentum,
    up_first,
    up_second,
    down_first,
    down_second,
):
    yl = (lax.axis_index("path") // 8) % 2
    live = (token_ids[0] != 0).astype(F32)[:, None]
    plane = lax.dynamic_index_in_dim(path_table.reshape(4, 2, 8, 2), yl, 1, keepdims=False)
    choice = jnp.repeat(plane.reshape(GROUP, 2).T, 16, axis=1)
    used = jnp.sum((path_table.T[:, None, :] == jnp.arange(C, dtype=jnp.int32)[None, :, None]).astype(F32), axis=2)
    coef = jnp.stack([1.0 / jnp.maximum(used, 1.0), 0.01 * jnp.minimum(used, 1.0)], axis=1).reshape(4 * C)
    anywhere = pl.BlockSpec(memory_space=pl.ANY)
    smem = pl.BlockSpec(memory_space=pltpu.SMEM)
    vmem = pl.BlockSpec(memory_space=pltpu.VMEM)
    dma = pltpu.SemaphoreType.DMA
    result = [jax.ShapeDtypeStruct(array.shape, F32) for array in (up_master, down_master, up_momentum, down_momentum)]
    return tuple(pl.pallas_call(
        kernel,
        out_shape=result,
        in_specs=[smem, smem, vmem, vmem] + [anywhere] * 10,
        out_specs=[anywhere] * 4,
        scratch_shapes=[
            pltpu.VMEM((C, 16, HALF_F), F32),
            pltpu.VMEM((C, 64, HALF_D), F32),
            pltpu.VMEM((C, 16, HALF_F), F32),
            pltpu.VMEM((C, 64, HALF_D), F32),
            pltpu.VMEM((TOK, D), BF16),
            pltpu.VMEM((TOK, D), BF16),
            pltpu.VMEM((C, 16, HALF_F), BF16),
            pltpu.VMEM((C, 16, HALF_F), BF16),
            pltpu.VMEM((C, 64, HALF_D), BF16),
            pltpu.VMEM((2, C, 64, HALF_D), BF16),
            pltpu.VMEM((2 * GROUP, 16, HALF_F), BF16),
            pltpu.VMEM((2 * GROUP, 64, HALF_D), BF16),
            pltpu.VMEM((2 * GROUP, 16, HALF_F), BF16),
            pltpu.VMEM((2, GROUP, 64, HALF_D), BF16),
            pltpu.VMEM((2, GROUP, 16, HALF_F), BF16),
            pltpu.VMEM((2, GROUP, 64, HALF_D), BF16),
            pltpu.VMEM((HALF_F, HALF_D), BF16),
            pltpu.VMEM((HALF_F, HALF_D), BF16),
            pltpu.VMEM((HALF_F, HALF_D), BF16),
            pltpu.VMEM((2 * TOK, D), BF16),
            pltpu.VMEM((2 * TOK, D), BF16),
            pltpu.VMEM((2, 8, 128), F32),
            pltpu.VMEM((2 * TOK, HALF_F), BF16),
            pltpu.VMEM((2, 2, 1024, 512), BF16),
            pltpu.VMEM((C, 16, HALF_F), BF16),
            pltpu.VMEM((C, 16, HALF_F), BF16),
            pltpu.VMEM((C, 64, HALF_D), BF16),
            pltpu.VMEM((C, 64, HALF_D), BF16),
            pltpu.VMEM((C * 16, GROUP * 16), BF16),
            pltpu.VMEM((C * 16, GROUP * 16), BF16),
            dma((6,)),
            dma((2, 2)),
            dma((4,)),
            dma((6,)),
            dma((6,)),
            dma((2,)),
            dma,
            dma,
            dma,
            dma,
            dma,
            dma((4,)),
            dma((4,)),
            dma,
            dma((2,)),
            dma,
            dma((2,)),
        ],
        compiler_params=pltpu.CompilerParams(
            collective_id=0, has_side_effects=True, vmem_limit_bytes=62 * 1024 * 1024
        ),
        cost_estimate=pl.CostEstimate(flops=12_884_901_888, bytes_accessed=30_000_000, transcendentals=1_572_864),
    )(
        path_table.reshape(-1),
        coef,
        choice,
        live,
        activations[0],
        cotangent[0],
        up_master,
        down_master,
        up_momentum,
        down_momentum,
        up_first[0],
        up_second[0],
        down_first[0],
        down_second[0],
    ))


def solution(mesh):
    placed = (
        P("path", "dp", None),
        P("path", "dp", None),
        P("path", "dp"),
        P(),
        P(None, "path", "dp"),
        P(None, "path", "dp"),
        P(None, "path", "dp"),
        P(None, "path", "dp"),
        P("path", None, "dp"),
        P("path", None, "dp"),
        P("path", None, "dp"),
        P("path", None, "dp"),
    )
    return jax.shard_map(
        shards,
        mesh=mesh,
        in_specs=placed,
        out_specs=(
            P(None, "path", "dp"),
            P(None, "path", "dp"),
            P(None, "path", "dp"),
            P(None, "path", "dp"),
        ),
        check_vma=False,
    )
```

time: 716 us -> 266 us (0.37)
  the two profiles are of different devices: /device:TPU:6 before, /device:TPU:56 now
where the time goes in v1:
time: 266 us
  Pallas kernels  252 us (95%)
  local copies, waits for them, and re-layouts  11.1 us (4%)
    pallas_call x1, Pallas kernels, shards(): pl.pallas_call(kernel, out_shape=result, in_specs=[smem, smem, vmem, vmem...  252 us
    unnamed x9, local copies, waits for them, and re-layouts  7.42 us

profile of v1, /device:TPU:56, one launch (start us, length us, event | category | flops | bytes accessed | tf_op | source)
XLA Modules:
  0.0 265.8 jit_solution(7694618879973187037)
XLA Ops:
  0.7 0.8 convert_reduce_fusion
  1.5 0.6 reshape.71.coef
  2.1 0.7 fusion
  2.7 0.8 reshape.72
  3.5 0.1 reshape.73
  3.6 0.1 broadcast_in_dim.2
  3.7 0.7 reshape.74.choice
  4.4 0.8 copy.21
  5.2 0.7 reshape.70.table
  5.8 0.8 copy.23.live
  6.6 252.5 %shard_map.147 = (f32[8,16,2048]{2,1,0:T(8,128)}, f32[8,64,512]{2,1,0:T(8,128)}, f32[8,16,2048]{2,1,0:T(8,128)}, f32[8,64,512]{2,1,0:T(8,128)}) custom-call(s32[128]{0:T(128)} %reshape.70.table, f32[32]{0:T(128)} %reshape.71.coef, s32[2,512]{1,0:T(2,128)} %reshape.74.choice, f32[384,1]{1,0:T(8,128)} %copy.23.live, bf16[384,1024]{1,0:T(8,128)(2,1)} %bitcast.24, ...), custom_call_target="tpu_custom_call" | custom-call | flops 12884901888 | bytes 30000000 | tf_op jit(solution)/shard_map/pallas_call | solution.py:466
  259.1 0.0 copy-start.1
  259.1 0.0 copy-start
  259.1 2.4 copy.28
  261.6 2.3 copy.29
  263.8 0.0 copy-done.1
  263.8 1.0 copy.30
  264.8 0.0 copy-done
  264.8 1.0 copy.31
  (4 shorter events, 0.1 us)
Async XLA Ops:
  259.1 4.7 %copy-start.1 = (f32[8,16,2048]{2,1,0:T(8,128)S(1)}, f32[8,16,2048]{2,1,0:T(8,128)}, u32[]{:S(2)}) copy-start(f32[8,16,2048]{2,1,0:T(8,128)} %get-tuple-element.12) | copy-start | bytes 3145732
  259.1 5.7 %copy-start = (f32[8,64,512]{2,1,0:T(8,128)S(1)}, f32[8,64,512]{2,1,0:T(8,128)}, u32[]{:S(2)}) copy-start(f32[8,64,512]{2,1,0:T(8,128)} %get-tuple-element.13) | copy-start | bytes 3145732

commit v2 on v1

--- a/solution.py
+++ b/solution.py
@@ -24,14 +24,17 @@
 def step_direction(gradient, first_moment, second_moment):
     first_new = 0.9 * first_moment.astype(F32) + 0.1 * gradient
     second_new = 0.95 * second_moment.astype(F32) + 0.05 * gradient * gradient
-    return (0.1 * first_new / (jnp.sqrt(second_new) + 1e-08)).astype(BF16)
+    below = second_new * lax.rsqrt(second_new) + 1e-08
+    over = pl.reciprocal(below, approx=True)
+    over = over * (2.0 - below * over)
+    return (0.1 * first_new * over).astype(BF16)
 
 
 def kernel(
-    table, coef, choice, live, act_in, cot_in, um_in, dm_in, umom_in, dmom_in, up_first, up_second,
-    down_first, down_second, um_out, dm_out, umom_out, dmom_out,
-    um, dm, umom, dmom, act, cot, upb, upf, dnb, blk, buf_a, buf_b, wup, wdn, rdn, rup,
-    gsend, gmine, grecv, nrm, og, count, gp, mom, pdn_send, pdn_recv, pup_send, pup_recv, pick_up, pick_dn,
+    table, ids, act_in, cot_in, um_in, dm_in, up_first, up_second, down_first, down_second, um_out, dm_out,
+    um, dm, act, cot, upb, upf, dnb, blk, buf_a, buf_b, wup, wdn, rdn, rup,
+    gsend, gmine, grecv, nrm, nrm_t, og, og_pass, count, used, gp, wide_a, act_a, wide_b, mom,
+    pdn_send, pdn_recv, pup_send, pup_recv, pick_t, pick_up, pick_dn,
     in_sem, mom_sem, out_sem, y_send, y_recv, dn_send, blk_recv, wu_send, wu_recv, wd_send, wd_recv,
     g_send, g_recv, dd_send, dd_recv, du_send, du_recv,
 ):
@@ -67,7 +70,7 @@
     loads = [
         pltpu.make_async_copy(src, dst, in_sem.at[i])
         for i, (src, dst) in enumerate(
-            [(um_in, um), (act_in, act), (dm_in, dm), (cot_in, cot), (umom_in, umom), (dmom_in, dmom)]
+            [(um_in, um), (act_in, act), (dm_in, dm), (cot_in, cot)]
         )
     ]
     for load in loads:
@@ -84,6 +87,7 @@
     lax.fori_loop(1, GROUP, greet, 0)
     for to_path, to_dp in (
         (place(x, other_yl, zc), here),
+        (place(x, other_yl, zc), there),
         (path, there),
         (place(3 - x, yl, zc), there),
         (place(3 - x, other_yl, zc), there),
@@ -92,7 +96,7 @@
 
     def pick_up_rows(side, source):
         def one(k, _):
-            module = table[2 * (lax.div(k, 8) * 16 + yl * 8 + lax.rem(k, 8))]
+            module = table[lax.div(k, 8) * 16 + yl * 8 + lax.rem(k, 8), 0]
             buf_a[side * GROUP + k] = source[module]
             return 0
 
@@ -101,7 +105,7 @@
     loads[0].wait()
     upb[...] = um[...].astype(BF16)
     pick_up_rows(yl, upb)
-    pl.semaphore_wait(barrier, GROUP + 3)
+    pl.semaphore_wait(barrier, GROUP + 4)
 
     up_swap = remote(upb, upf, y_send.at[0], y_recv.at[0], place(x, other_yl, zc), here)
     up_swap.start()
@@ -149,42 +153,38 @@
         pltpu.make_async_copy(dnb, blk.at[yl], blk_recv).start()
 
     loads[3].wait()
+    live = jnp.sum((ids[...] != 0).astype(F32))
     for part in range(3):
         rows = pl.ds(part * 128, 128)
         to_rows = pl.ds(pl.multiple_of(here * TOK + part * 128, 128), 128)
-        og[to_rows, :] = (cot[rows, :].astype(F32) * live[rows, :]).astype(BF16)
-    count[0] = jnp.broadcast_to(jnp.sum(live[...]), (8, 128))
-    og_swap = remote(og.at[own_rows], og.at[own_rows], y_send.at[2], y_recv.at[2], path, there)
-    og_swap.start()
+        position = (lax.broadcasted_iota(jnp.int32, (128, D), 0) + part * 128).astype(F32)
+        og[to_rows, :] = jnp.where(position < live, cot[rows, :].astype(F32), 0.0).astype(BF16)
+    count[0] = jnp.broadcast_to(live, (8, 128))
     count_swap = remote(count.at[0], count.at[1], y_send.at[3], y_recv.at[3], path, there)
     count_swap.start()
+    dp_below = lax.rem(here + other_yl, 2)
+    below = place(x, other_yl, zc)
+    og_first = remote(og.at[own_rows], og_pass, y_send.at[2], y_recv.at[2], below, dp_below)
+    og_first.start()
 
     up_swap.wait()
     pick_up_rows(other_yl, upf)
     send_up_rows(other_yl)
 
+    og_first.wait()
+    pass_rows = pl.ds(pl.multiple_of((1 - dp_below) * TOK, TOK), TOK)
+    og_second = remote(og_pass, og.at[pass_rows], y_send.at[6], y_recv.at[6], below, dp_below)
+    og_second.start()
+
     settle(blk, blk_recv)
 
     def pick_down_rows(k, _):
-        module = table[2 * (lax.div(k, 8) * 16 + yl * 8 + lax.rem(k, 8)) + 1]
+        module = table[lax.div(k, 8) * 16 + yl * 8 + lax.rem(k, 8), 1]
         buf_b[k] = blk[0, module]
         buf_b[GROUP + k] = blk[1, module]
         return 0
 
     lax.fori_loop(0, GROUP, pick_down_rows, 0)
-
-    nrm_swap.wait()
-    og_swap.wait()
-    count_swap.wait()
-    per_count = 1.0 / (count[0] + count[1])
-    per_count = per_count[0:1, 0:1]
-
-    def scale_rows(i, _):
-        rows = pl.ds(pl.multiple_of(i * 64, 64), 64)
-        og[rows, :] = (og[rows, :].astype(F32) * per_count).astype(BF16)
-        return 0
-
-    lax.fori_loop(0, 12, scale_rows, 0)
 
     settle(buf_a.at[pl.ds(0, 2 * GROUP - 2)], wu_send)
     from_x = x_to - 2 * here
@@ -202,11 +202,36 @@
 
         lax.fori_loop(1, GROUP, one, 0)
 
+    nrm_swap.wait()
+
+    def turn(i, _):
+        cols = pl.ds(pl.multiple_of(i * 256, 256), 256)
+        nrm_t[cols, :] = nrm[:, cols].T
+        return 0
+
+    lax.fori_loop(0, 4, turn, 0)
+    count_swap.wait()
+    per_count = 1.0 / (count[0] + count[1])
+    per_count = per_count[0:1, 0:1]
+    og_second.wait()
+
+    def scale_rows(i, _):
+        rows = pl.ds(pl.multiple_of(i * 64, 64), 64)
+        og[rows, :] = (og[rows, :].astype(F32) * per_count).astype(BF16)
+        return 0
+
+    lax.fori_loop(0, 12, scale_rows, 0)
+
     down_x = [here * 2 + lax.rem(x + i, 2) for i in range(2)] + [there * 2 + lax.rem(x + i, 2) for i in range(2)]
     up_x = [lax.rem(x + i, 4) for i in (2, 1, 3, 0)]
 
-    def fetch(step):
-        slot = step % 2
+    order = (0, 1, 4, 5, 6, 7, 2, 3)
+
+    def fetch(turn_no):
+        if turn_no >= 8:
+            return
+        slot = turn_no % 2
+        step = order[turn_no]
         for kind, (down_source, up_source) in enumerate(((down_first, up_first), (down_second, up_second))):
             if step < 4:
                 rows = pl.ds(pl.multiple_of(down_x[step] * 1024, 1024), 1024)
@@ -222,8 +247,8 @@
                         mom_sem.at[slot, kind],
                     ).start()
 
-    def await_moments(step):
-        slot = step % 2
+    def await_moments(turn_no):
+        slot = turn_no % 2
         for kind in range(2):
             settle(mom.at[slot, kind], mom_sem.at[slot, kind])
 
@@ -238,50 +263,63 @@
         rows = pl.ds(pl.multiple_of(chunk * 512, 512), 512)
         return remote(gsend.at[rows], grecv.at[rows], g_send.at[chunk], g_recv.at[chunk], path, there)
 
-    def hidden(i, _):
+    def pre_act(i, half):
         cols = pl.ds(pl.multiple_of(i * 256, 256), 256)
         weights = wup[:, :, cols].reshape(D, 256)
-        pre = jnp.dot(nrm[...], weights, preferred_element_type=F32) * UP_SCALE
-        sig = 0.5 * jnp.tanh(0.5 * pre) + 0.5
-        out = (pre * sig).astype(BF16)
-        gp[:, cols] = (sig * (1.0 + pre * (1.0 - sig))).astype(BF16)
-        theirs = lax.dot_general(out, og[:, their_cols], TN, preferred_element_type=F32)
-        gsend[cols, :] = (theirs * DOWN_SCALE).astype(BF16)
-
-        @pl.when(lax.rem(i, 2) == 1)
-        def _():
-            g_copy(lax.div(i, 2)).start()
-
-        mine = lax.dot_general(out, og[:, mine_cols], TN, preferred_element_type=F32)
-        gmine[cols, :] = (mine * DOWN_SCALE).astype(BF16)
+        wide_a[half] = jnp.dot(nrm[...], weights, preferred_element_type=F32)
+
+    pre_act(0, 0)
+
+    def hidden(pair, _):
+        for half in range(2):
+            i = pair * 2 + half
+            pre_act(jnp.minimum(i + 1, 7), 1 - half)
+            cols = pl.ds(pl.multiple_of(i * 256, 256), 256)
+            for strip in range(24):
+                rows = pl.ds(strip * 32, 32)
+                pre = wide_a[half, rows, :] * UP_SCALE
+                sig = 0.5 * jnp.tanh(0.5 * pre) + 0.5
+                out = pre * sig
+                act_a[half, rows, :] = out.astype(BF16)
+                gp[rows, cols] = (sig + out * (1.0 - sig)).astype(BF16)
+            out_t = act_a[half].T
+            theirs = jnp.dot(out_t, og[:, their_cols], preferred_element_type=F32)
+            gsend[cols, :] = (theirs * DOWN_SCALE).astype(BF16)
+            if half == 1:
+                g_copy(pair).start()
+            mine = jnp.dot(out_t, og[:, mine_cols], preferred_element_type=F32)
+            gmine[cols, :] = (mine * DOWN_SCALE).astype(BF16)
         return 0
 
-    lax.fori_loop(0, 8, hidden, 0)
-
-    def down_step(step):
+    lax.fori_loop(0, 4, hidden, 0)
+
+    def down_delta(turn_no):
+        step = order[turn_no]
         x_ = down_x[step]
         source = gmine if step < 2 else grecv
         first_row = lax.rem(x_, 2) * 1024
         if step >= 2:
             for half in range(2):
                 g_copy(lax.rem(x_, 2) * 2 + half).wait_recv()
-        await_moments(step)
-        slot = step % 2
+        await_moments(turn_no)
+        slot = turn_no % 2
 
         def one(q, _):
-            rows = pl.ds(pl.multiple_of(q * 64, 64), 64)
-            grad = source[pl.ds(pl.multiple_of(first_row + q * 64, 64), 64), :].astype(F32)
-            delta = step_direction(grad, mom[slot, 0, rows, :], mom[slot, 1, rows, :])
             for b in range(4):
-                buf_a[x_ * 16 + q, :, pl.ds(b * 512, 512)] = delta[b * 16 : b * 16 + 16, :]
+                rows = pl.ds(pl.multiple_of(q * 64 + b * 16, 16), 16)
+                grad = source[pl.ds(pl.multiple_of(first_row + q * 64 + b * 16, 16), 16), :].astype(F32)
+                delta = step_direction(grad, mom[slot, 0, rows, :], mom[slot, 1, rows, :])
+                buf_a[x_ * 16 + q, :, pl.ds(b * 512, 512)] = delta
             return 0
 
         lax.fori_loop(0, 16, one, 0)
-        fetch(step + 2)
+        fetch(turn_no + 2)
+
+    def send_down_delta(step, side):
+        x_ = down_x[step]
 
         def send(k, _):
-            zc_ = zc_at(lax.rem(k, 8))
-            side = lax.rem(other_yl + lax.div(k, 8), 2)
+            zc_ = zc_at(k)
             row = x_ * 16 + side * 8 + zc_
             away = (x_ * 8 + zc_) != group
 
@@ -297,10 +335,12 @@
 
             return 0
 
-        lax.fori_loop(0, 16, send, 0)
-
-    down_step(0)
-    down_step(1)
+        lax.fori_loop(0, 8, send, 0)
+
+    for turn_no in range(2):
+        down_delta(turn_no)
+        send_down_delta(turn_no, other_yl)
+        send_down_delta(turn_no, yl)
 
     settle(wdn, wd_recv)
 
@@ -315,8 +355,6 @@
 
     lax.fori_loop(0, 8, hidden_grad, 0)
     settle(buf_b.at[pl.ds(0, 2 * GROUP - 2)], wd_send)
-    down_step(2)
-    down_step(3)
 
     def send_up_delta(x_, zc_, side):
         row = x_ * 16 + side * 8 + zc_
@@ -332,23 +370,25 @@
         def _():
             pltpu.make_async_copy(buf_b.at[row], rup.at[side, group], du_recv.at[side]).start()
 
-    def up_step(step):
-        x_ = up_x[step - 4]
-        await_moments(step)
-        slot = step % 2
-        lhs = nrm[:, pl.ds(pl.multiple_of(x_ * 256, 256), 256)]
-
-        def one(b, _):
-            cols = pl.ds(pl.multiple_of(b * 512, 512), 512)
-            rows = pl.ds(pl.multiple_of(b * 256, 256), 256)
-            grad = lax.dot_general(lhs, gp[:, cols], TN, preferred_element_type=F32) * UP_SCALE
-            delta = step_direction(grad, mom[slot, 0, rows, :], mom[slot, 1, rows, :])
-            buf_b[pl.ds(x_ * 16, 16), pl.ds(pl.multiple_of(b * 16, 16), 16), :] = delta.reshape(16, 16, 512)
-            return 0
-
-        lax.fori_loop(0, 4, one, 0)
-        if step + 2 < 8:
-            fetch(step + 2)
+    def up_step(turn_no):
+        x_ = up_x[order[turn_no] - 4]
+        slot = turn_no % 2
+        lhs = nrm_t[pl.ds(pl.multiple_of(x_ * 256, 256), 256), :]
+
+        def up_grad(b):
+            wide_b[b % 2] = jnp.dot(lhs, gp[:, pl.ds(b * 512, 512)], preferred_element_type=F32)
+
+        up_grad(0)
+        await_moments(turn_no)
+        for b in range(4):
+            if b < 3:
+                up_grad(b + 1)
+            for i in range(16):
+                rows = pl.ds(b * 256 + i * 16, 16)
+                grad = wide_b[b % 2, pl.ds(i * 16, 16), :] * UP_SCALE
+                delta = step_direction(grad, mom[slot, 0, rows, :], mom[slot, 1, rows, :])
+                buf_b[x_ * 16 + i, pl.ds(b * 16, 16), :] = delta
+        fetch(turn_no + 2)
 
         def send(k, _):
             send_up_delta(x_, zc_at(k), other_yl)
@@ -356,8 +396,8 @@
 
         lax.fori_loop(0, 8, send, 0)
 
-    for step in range(4, 8):
-        up_step(step)
+    for turn_no in range(2, 6):
+        up_step(turn_no)
 
     def send_rest(k, _):
         x_, zc_ = peer(lax.rem(k * 11, GROUP))
@@ -366,12 +406,32 @@
 
     lax.fori_loop(0, GROUP, send_rest, 0)
 
-    module_row = lax.broadcasted_iota(jnp.int32, (C * 16, GROUP * 16), 0)
-    path_row = lax.broadcasted_iota(jnp.int32, (C * 16, GROUP * 16), 1)
-    same_row = (module_row & 15) == (path_row & 15)
-    module = module_row >> 4
-    pick_up[...] = jnp.where(same_row & (module == choice[0:1, :]), 1.0, 0.0).astype(BF16)
-    pick_dn[...] = jnp.where(same_row & (module == choice[1:2, :]), 1.0, 0.0).astype(BF16)
+    for turn_no in range(6, 8):
+        down_delta(turn_no)
+        send_down_delta(order[turn_no], other_yl)
+    for turn_no in range(6, 8):
+        send_down_delta(order[turn_no], yl)
+
+    lane = lax.broadcasted_iota(jnp.int32, (16, C * 16), 1)
+    same_row = (lane & 15) == lax.broadcasted_iota(jnp.int32, (16, C * 16), 0)
+    for level, pick in enumerate((pick_up, pick_dn)):
+
+        def fill(k, _, level=level):
+            module = table[lax.div(k, 8) * 16 + yl * 8 + lax.rem(k, 8), level]
+            rows = pl.ds(pl.multiple_of(k * 16, 16), 16)
+            pick_t[rows, :] = jnp.where(same_row & ((lane >> 4) == module), 1.0, 0.0)
+            return 0
+
+        lax.fori_loop(0, GROUP, fill, 0)
+        pick[...] = pick_t[...].T.astype(BF16)
+
+        def tally(k, counts, level=level):
+            module = table[k, level]
+            return tuple(n + jnp.where(module == m, 1, 0) for m, n in enumerate(counts))
+
+        counts = lax.fori_loop(0, 64, tally, (jnp.int32(0),) * C)
+        for m in range(C):
+            used[level * C + m] = counts[m]
 
     def down_sum(side, b):
         block = rdn[side, :, :, pl.ds(b * 512, 512)].reshape(GROUP * 16, 512)
@@ -381,35 +441,18 @@
         block = rup[side, :, pl.ds(b * 16, 16), :].reshape(GROUP * 16, 512)
         return jnp.dot(pick_up[...], block, preferred_element_type=F32).reshape(C, 16, 512)
 
-    def finish(total, master, momentum, level, rows, cols):
+    def finish(total, master, level, rows, cols):
         for m in range(C):
-            weights = master[m, rows, cols]
-            mean = total[m] * coef[level * 16 + m] + coef[level * 16 + 8 + m] * weights.astype(BF16).astype(F32)
-            speed = 0.9 * momentum[m, rows, cols] + mean
-            momentum[m, rows, cols] = speed
-            master[m, rows, cols] = weights - 0.7 * (mean + 0.9 * speed)
+            number = jnp.broadcast_to(used[level * C + m].astype(F32), (8, 128))
+            per_used = (1.0 / jnp.maximum(number, 1.0))[0:1, 0:1]
+            decay = (0.01 * jnp.minimum(number, 1.0))[0:1, 0:1]
+            weights = master[m, rows, cols].astype(BF16).astype(F32)
+            master[m, rows, cols] = total[m] * per_used + decay * weights
 
     mate = place(x, other_yl, zc)
-    settle(rdn.at[other_yl], dd_recv.at[other_yl])
-    for b in range(4):
-        pdn_send[:, :, pl.ds(b * 512, 512)] = down_sum(other_yl, b).astype(BF16)
-    dn_part = remote(pdn_send, pdn_recv, y_send.at[4], y_recv.at[4], mate, here)
-    dn_part.start()
-    settle(rdn.at[yl], dd_recv.at[yl])
-    for load in loads[4:]:
-        load.wait()
-    dn_part.wait()
-    for b in range(4):
-        cols = pl.ds(b * 512, 512)
-        total = down_sum(yl, b) + pdn_recv[:, :, cols].astype(F32)
-        finish(total, dm, dmom, 1, pl.ds(b * 16, 16), pl.ds(0, 512))
     stores = [
-        pltpu.make_async_copy(src, dst, out_sem.at[i])
-        for i, (src, dst) in enumerate([(dm, dm_out), (dmom, dmom_out), (um, um_out), (umom, umom_out)])
+        pltpu.make_async_copy(src, dst, out_sem.at[i]) for i, (src, dst) in enumerate([(dm, dm_out), (um, um_out)])
     ]
-    stores[0].start()
-    stores[1].start()
-
     settle(rup.at[other_yl], du_recv.at[other_yl])
     for b in range(4):
         pup_send[:, pl.ds(b * 16, 16), :] = up_sum(other_yl, b).astype(BF16)
@@ -420,9 +463,21 @@
     for b in range(4):
         rows = pl.ds(b * 16, 16)
         total = up_sum(yl, b) + pup_recv[:, rows, :].astype(F32)
-        finish(total, um, umom, 0, pl.ds(0, 16), pl.ds(b * 512, 512))
-    stores[2].start()
-    stores[3].start()
+        finish(total, um, 0, pl.ds(0, 16), pl.ds(b * 512, 512))
+    stores[1].start()
+
+    settle(rdn.at[other_yl], dd_recv.at[other_yl])
+    for b in range(4):
+        pdn_send[:, :, pl.ds(b * 512, 512)] = down_sum(other_yl, b).astype(BF16)
+    dn_part = remote(pdn_send, pdn_recv, y_send.at[4], y_recv.at[4], mate, here)
+    dn_part.start()
+    settle(rdn.at[yl], dd_recv.at[yl])
+    dn_part.wait()
+    for b in range(4):
+        cols = pl.ds(b * 512, 512)
+        total = down_sum(yl, b) + pdn_recv[:, :, cols].astype(F32)
+        finish(total, dm, 1, pl.ds(b * 16, 16), pl.ds(0, 512))
+    stores[0].start()
 
     dn_far.wait_send()
 
@@ -452,25 +507,16 @@
     down_first,
     down_second,
 ):
-    yl = (lax.axis_index("path") // 8) % 2
-    live = (token_ids[0] != 0).astype(F32)[:, None]
-    plane = lax.dynamic_index_in_dim(path_table.reshape(4, 2, 8, 2), yl, 1, keepdims=False)
-    choice = jnp.repeat(plane.reshape(GROUP, 2).T, 16, axis=1)
-    used = jnp.sum((path_table.T[:, None, :] == jnp.arange(C, dtype=jnp.int32)[None, :, None]).astype(F32), axis=2)
-    coef = jnp.stack([1.0 / jnp.maximum(used, 1.0), 0.01 * jnp.minimum(used, 1.0)], axis=1).reshape(4 * C)
     anywhere = pl.BlockSpec(memory_space=pl.ANY)
     smem = pl.BlockSpec(memory_space=pltpu.SMEM)
     vmem = pl.BlockSpec(memory_space=pltpu.VMEM)
     dma = pltpu.SemaphoreType.DMA
-    result = [jax.ShapeDtypeStruct(array.shape, F32) for array in (up_master, down_master, up_momentum, down_momentum)]
-    return tuple(pl.pallas_call(
+    up_mean, down_mean = pl.pallas_call(
         kernel,
-        out_shape=result,
-        in_specs=[smem, smem, vmem, vmem] + [anywhere] * 10,
-        out_specs=[anywhere] * 4,
+        out_shape=[jax.ShapeDtypeStruct(array.shape, F32) for array in (up_master, down_master)],
+        in_specs=[smem, vmem] + [anywhere] * 8,
+        out_specs=[anywhere] * 2,
         scratch_shapes=[
-            pltpu.VMEM((C, 16, HALF_F), F32),
-            pltpu.VMEM((C, 64, HALF_D), F32),
             pltpu.VMEM((C, 16, HALF_F), F32),
             pltpu.VMEM((C, 64, HALF_D), F32),
             pltpu.VMEM((TOK, D), BF16),
@@ -489,21 +535,28 @@
             pltpu.VMEM((HALF_F, HALF_D), BF16),
             pltpu.VMEM((HALF_F, HALF_D), BF16),
             pltpu.VMEM((2 * TOK, D), BF16),
+            pltpu.VMEM((D, 2 * TOK), BF16),
             pltpu.VMEM((2 * TOK, D), BF16),
+            pltpu.VMEM((TOK, D), BF16),
             pltpu.VMEM((2, 8, 128), F32),
+            pltpu.SMEM((2 * C,), jnp.int32),
             pltpu.VMEM((2 * TOK, HALF_F), BF16),
+            pltpu.VMEM((2, 2 * TOK, 256), F32),
+            pltpu.VMEM((2, 2 * TOK, 256), BF16),
+            pltpu.VMEM((2, 256, 512), F32),
             pltpu.VMEM((2, 2, 1024, 512), BF16),
             pltpu.VMEM((C, 16, HALF_F), BF16),
             pltpu.VMEM((C, 16, HALF_F), BF16),
             pltpu.VMEM((C, 64, HALF_D), BF16),
             pltpu.VMEM((C, 64, HALF_D), BF16),
+            pltpu.VMEM((GROUP * 16, C * 16), F32),
             pltpu.VMEM((C * 16, GROUP * 16), BF16),
             pltpu.VMEM((C * 16, GROUP * 16), BF16),
-            dma((6,)),
+            dma((4,)),
             dma((2, 2)),
-            dma((4,)),
-            dma((6,)),
-            dma((6,)),
+            dma((2,)),
+            dma((7,)),
+            dma((7,)),
             dma((2,)),
             dma,
             dma,
@@ -522,21 +575,22 @@
         ),
         cost_estimate=pl.CostEstimate(flops=12_884_901_888, bytes_accessed=30_000_000, transcendentals=1_572_864),
     )(
-        path_table.reshape(-1),
-        coef,
-        choice,
-        live,
+        path_table,
+        token_ids,
         activations[0],
         cotangent[0],
         up_master,
         down_master,
-        up_momentum,
-        down_momentum,
         up_first[0],
         up_second[0],
         down_first[0],
         down_second[0],
-    ))
+    )
+    new_up_momentum = 0.9 * up_momentum + up_mean
+    new_down_momentum = 0.9 * down_momentum + down_mean
+    new_up_master = up_master - 0.7 * (up_mean + 0.9 * new_up_momentum)
+    new_down_master = down_master - 0.7 * (down_mean + 0.9 * new_down_momentum)
+    return (new_up_master, new_down_master, new_up_momentum, new_down_momentum)
 
 
 def solution(mesh):

time: 266 us -> 262 us (0.985)
  the two profiles are of different devices: /device:TPU:56 before, /device:TPU:6 now
where the time goes in v2:
time: 262 us; the launch traced here: 257 us
  Pallas kernels  250 us (95%)
  other arithmetic  5.12 us (2%)
    pallas_call x1, Pallas kernels, shards(): pl.pallas_call(kernel, out_shape=[jax.ShapeDtypeStruct(array.shape, F32)...  250 us

profile of v2, /device:TPU:6, one launch (start us, length us, event | category | flops | bytes accessed | tf_op | source)
XLA Modules:
  0.0 256.9 jit_solution(5669057159320420684)
XLA Ops:
  0.6 1.4 copy.16.table
  2.0 0.0 copy-start
  2.0 249.7 %shard_map.147 = (f32[8,16,2048]{2,1,0:T(8,128)}, f32[8,64,512]{2,1,0:T(8,128)}) custom-call(s32[64,2]{1,0:T(8,128)} %copy.16.table, s32[1,384]{1,0:T(1,128)} %ids.1, bf16[384,1024]{1,0:T(8,128)(2,1)} %bitcast.10, bf16[384,1024]{1,0:T(8,128)(2,1)} %bitcast.11, f32[8,16,2048]{2,1,0:T(8,128)} %um_in.1, f32[8,64,512]{2,1,0:T(8,128)} %dm_in.1, ...), custom_call_target="tpu_custom_call" | custom-call | flops 12884901888 | bytes 30000000 | tf_op jit(solution)/shard_map/pallas_call | solution.py:514
  251.7 0.0 copy-start.1
  251.7 0.0 copy-start.2
  251.7 0.0 copy-start.3
  251.7 0.0 copy-done
  251.7 3.4 %multiply_subtract_fusion.1 = (f32[8,16,2048]{2,1,0:T(8,128)}, f32[8,16,2048]{2,1,0:T(8,128)}) fusion(f32[8,16,2048]{2,1,0:T(8,128)S(1)} %copy-done, f32[8,16,2048]{2,1,0:T(8,128)} %get-tuple-element.6, f32[8,16,2048]{2,1,0:T(8,128)} %param.18), kind=kLoop, calls=%fused_computation.2 | loop fusion | flops 1572864 | bytes 5242880 | tf_op jit(solution)/shard_map/sub | solution.py:591
  255.2 0.0 copy-done.1
  255.2 0.0 copy-done.2
  255.2 0.0 copy-done.3
  255.2 1.7 multiply_subtract_fusion
Async XLA Ops:
  2.0 249.7 %copy-start = (f32[8,16,2048]{2,1,0:T(8,128)S(1)}, f32[8,16,2048]{2,1,0:T(8,128)}, u32[]{:S(2)}) copy-start(f32[8,16,2048]{2,1,0:T(8,128)} %um_in.1) | copy-start | bytes 3145732
  251.7 3.5 %copy-start.1 = (f32[8,64,512]{2,1,0:T(8,128)S(1)}, f32[8,64,512]{2,1,0:T(8,128)}, u32[]{:S(2)}) copy-start(f32[8,64,512]{2,1,0:T(8,128)} %dm_in.1) | copy-start | bytes 3145732
  251.7 3.5 %copy-start.2 = (f32[8,64,512]{2,1,0:T(8,128)S(1)}, f32[8,64,512]{2,1,0:T(8,128)}, u32[]{:S(2)}) copy-start(f32[8,64,512]{2,1,0:T(8,128)} %param.19) | copy-start | bytes 3145732
  251.7 3.4 %copy-start.3 = (f32[8,64,512]{2,1,0:T(8,128)S(1)}, f32[8,64,512]{2,1,0:T(8,128)}, u32[]{:S(2)}) copy-start(f32[8,64,512]{2,1,0:T(8,128)} %get-tuple-element.7) | copy-start | bytes 3145732

commit v3 on v2

--- a/solution.py
+++ b/solution.py
@@ -33,7 +33,7 @@
 def kernel(
     table, ids, act_in, cot_in, um_in, dm_in, up_first, up_second, down_first, down_second, um_out, dm_out,
     um, dm, act, cot, upb, upf, dnb, blk, buf_a, buf_b, wup, wdn, rdn, rup,
-    gsend, gmine, grecv, nrm, nrm_t, og, og_pass, count, used, gp, wide_a, act_a, wide_b, mom,
+    gsend, gmine, grecv, nrm, nrm_t, og, count, used, gp, wide_a, act_a, wide_b, mom,
     pdn_send, pdn_recv, pup_send, pup_recv, pick_t, pick_up, pick_dn,
     in_sem, mom_sem, out_sem, y_send, y_recv, dn_send, blk_recv, wu_send, wu_recv, wd_send, wd_recv,
     g_send, g_recv, dd_send, dd_recv, du_send, du_recv,
@@ -87,7 +87,6 @@
     lax.fori_loop(1, GROUP, greet, 0)
     for to_path, to_dp in (
         (place(x, other_yl, zc), here),
-        (place(x, other_yl, zc), there),
         (path, there),
         (place(3 - x, yl, zc), there),
         (place(3 - x, other_yl, zc), there),
@@ -105,25 +104,25 @@
     loads[0].wait()
     upb[...] = um[...].astype(BF16)
     pick_up_rows(yl, upb)
-    pl.semaphore_wait(barrier, GROUP + 4)
+    pl.semaphore_wait(barrier, GROUP + 3)
 
     up_swap = remote(upb, upf, y_send.at[0], y_recv.at[0], place(x, other_yl, zc), here)
     up_swap.start()
 
-    def send_up_rows(side):
+    def send_up_rows(side, half):
         row = place(x, side, zc)
         pltpu.make_async_copy(buf_a.at[side * GROUP + group], wup.at[row], wu_recv).start()
 
         def one(k, _):
             x_, zc_ = peer(lax.rem(k * 11, GROUP))
             remote(
-                buf_a.at[side * GROUP + x_ * 8 + zc_], wup.at[row], wu_send, wu_recv, place(x_, yl, zc_), here
+                buf_a.at[side * GROUP + x_ * 8 + zc_], wup.at[row], wu_send.at[half], wu_recv, place(x_, yl, zc_), here
             ).start()
             return 0
 
         lax.fori_loop(1, GROUP, one, 0)
 
-    send_up_rows(yl)
+    send_up_rows(yl, 0)
 
     own_rows = pl.ds(pl.multiple_of(here * TOK, TOK), TOK)
     loads[1].wait()
@@ -162,19 +161,12 @@
     count[0] = jnp.broadcast_to(live, (8, 128))
     count_swap = remote(count.at[0], count.at[1], y_send.at[3], y_recv.at[3], path, there)
     count_swap.start()
-    dp_below = lax.rem(here + other_yl, 2)
-    below = place(x, other_yl, zc)
-    og_first = remote(og.at[own_rows], og_pass, y_send.at[2], y_recv.at[2], below, dp_below)
-    og_first.start()
+    og_swap = remote(og.at[own_rows], og.at[own_rows], y_send.at[2], y_recv.at[2], path, there)
+    og_swap.start()
 
     up_swap.wait()
     pick_up_rows(other_yl, upf)
-    send_up_rows(other_yl)
-
-    og_first.wait()
-    pass_rows = pl.ds(pl.multiple_of((1 - dp_below) * TOK, TOK), TOK)
-    og_second = remote(og_pass, og.at[pass_rows], y_send.at[6], y_recv.at[6], below, dp_below)
-    og_second.start()
+    send_up_rows(other_yl, 1)
 
     settle(blk, blk_recv)
 
@@ -186,7 +178,7 @@
 
     lax.fori_loop(0, GROUP, pick_down_rows, 0)
 
-    settle(buf_a.at[pl.ds(0, 2 * GROUP - 2)], wu_send)
+    settle(buf_a.at[pl.ds(0, GROUP - 1)], wu_send.at[0])
     from_x = x_to - 2 * here
     for side in range(2):
         row = from_x * 16 + side * 8 + zc
@@ -213,7 +205,7 @@
     count_swap.wait()
     per_count = 1.0 / (count[0] + count[1])
     per_count = per_count[0:1, 0:1]
-    og_second.wait()
+    og_swap.wait()
 
     def scale_rows(i, _):
         rows = pl.ds(pl.multiple_of(i * 64, 64), 64)
@@ -225,7 +217,7 @@
     down_x = [here * 2 + lax.rem(x + i, 2) for i in range(2)] + [there * 2 + lax.rem(x + i, 2) for i in range(2)]
     up_x = [lax.rem(x + i, 4) for i in (2, 1, 3, 0)]
 
-    order = (0, 1, 4, 5, 6, 7, 2, 3)
+    order = (0, 1, 2, 3, 4, 5, 6, 7)
 
     def fetch(turn_no):
         if turn_no >= 8:
@@ -268,12 +260,13 @@
         weights = wup[:, :, cols].reshape(D, 256)
         wide_a[half] = jnp.dot(nrm[...], weights, preferred_element_type=F32)
 
-    pre_act(0, 0)
+    first_tile = 4 * lax.rem(x, 2)
+    pre_act(first_tile, 0)
 
     def hidden(pair, _):
         for half in range(2):
-            i = pair * 2 + half
-            pre_act(jnp.minimum(i + 1, 7), 1 - half)
+            i = lax.rem(first_tile + pair * 2 + half, 8)
+            pre_act(lax.rem(i + 1, 8), 1 - half)
             cols = pl.ds(pl.multiple_of(i * 256, 256), 256)
             for strip in range(24):
                 rows = pl.ds(strip * 32, 32)
@@ -286,7 +279,7 @@
             theirs = jnp.dot(out_t, og[:, their_cols], preferred_element_type=F32)
             gsend[cols, :] = (theirs * DOWN_SCALE).astype(BF16)
             if half == 1:
-                g_copy(pair).start()
+                g_copy(lax.div(i, 2)).start()
             mine = jnp.dot(out_t, og[:, mine_cols], preferred_element_type=F32)
             gmine[cols, :] = (mine * DOWN_SCALE).astype(BF16)
         return 0
@@ -337,7 +330,8 @@
 
         lax.fori_loop(0, 8, send, 0)
 
-    for turn_no in range(2):
+    settle(buf_a.at[pl.ds(0, GROUP - 1)], wu_send.at[1])
+    for turn_no in range(4):
         down_delta(turn_no)
         send_down_delta(turn_no, other_yl)
         send_down_delta(turn_no, yl)
@@ -396,7 +390,7 @@
 
         lax.fori_loop(0, 8, send, 0)
 
-    for turn_no in range(2, 6):
+    for turn_no in range(4, 8):
         up_step(turn_no)
 
     def send_rest(k, _):
@@ -405,12 +399,6 @@
         return 0
 
     lax.fori_loop(0, GROUP, send_rest, 0)
-
-    for turn_no in range(6, 8):
-        down_delta(turn_no)
-        send_down_delta(order[turn_no], other_yl)
-    for turn_no in range(6, 8):
-        send_down_delta(order[turn_no], yl)
 
     lane = lax.broadcasted_iota(jnp.int32, (16, C * 16), 1)
     same_row = (lane & 15) == lax.broadcasted_iota(jnp.int32, (16, C * 16), 0)
@@ -453,6 +441,19 @@
     stores = [
         pltpu.make_async_copy(src, dst, out_sem.at[i]) for i, (src, dst) in enumerate([(dm, dm_out), (um, um_out)])
     ]
+    settle(rdn.at[other_yl], dd_recv.at[other_yl])
+    for b in range(4):
+        pdn_send[:, :, pl.ds(b * 512, 512)] = down_sum(other_yl, b).astype(BF16)
+    dn_part = remote(pdn_send, pdn_recv, y_send.at[4], y_recv.at[4], mate, here)
+    dn_part.start()
+    settle(rdn.at[yl], dd_recv.at[yl])
+    dn_part.wait()
+    for b in range(4):
+        cols = pl.ds(b * 512, 512)
+        total = down_sum(yl, b) + pdn_recv[:, :, cols].astype(F32)
+        finish(total, dm, 1, pl.ds(b * 16, 16), pl.ds(0, 512))
+    stores[0].start()
+
     settle(rup.at[other_yl], du_recv.at[other_yl])
     for b in range(4):
         pup_send[:, pl.ds(b * 16, 16), :] = up_sum(other_yl, b).astype(BF16)
@@ -465,19 +466,6 @@
         total = up_sum(yl, b) + pup_recv[:, rows, :].astype(F32)
         finish(total, um, 0, pl.ds(0, 16), pl.ds(b * 512, 512))
     stores[1].start()
-
-    settle(rdn.at[other_yl], dd_recv.at[other_yl])
-    for b in range(4):
-        pdn_send[:, :, pl.ds(b * 512, 512)] = down_sum(other_yl, b).astype(BF16)
-    dn_part = remote(pdn_send, pdn_recv, y_send.at[4], y_recv.at[4], mate, here)
-    dn_part.start()
-    settle(rdn.at[yl], dd_recv.at[yl])
-    dn_part.wait()
-    for b in range(4):
-        cols = pl.ds(b * 512, 512)
-        total = down_sum(yl, b) + pdn_recv[:, :, cols].astype(F32)
-        finish(total, dm, 1, pl.ds(b * 16, 16), pl.ds(0, 512))
-    stores[0].start()
 
     dn_far.wait_send()
 
@@ -537,7 +525,6 @@
             pltpu.VMEM((2 * TOK, D), BF16),
             pltpu.VMEM((D, 2 * TOK), BF16),
             pltpu.VMEM((2 * TOK, D), BF16),
-            pltpu.VMEM((TOK, D), BF16),
             pltpu.VMEM((2, 8, 128), F32),
             pltpu.SMEM((2 * C,), jnp.int32),
             pltpu.VMEM((2 * TOK, HALF_F), BF16),
@@ -555,11 +542,11 @@
             dma((4,)),
             dma((2, 2)),
             dma((2,)),
-            dma((7,)),
-            dma((7,)),
+            dma((6,)),
+            dma((6,)),
             dma((2,)),
             dma,
-            dma,
+            dma((2,)),
             dma,
             dma,
             dma,

time: 262 us -> 249 us (0.950); the launches traced: 257 us -> 249 us
  Pallas kernels: 250 us -> 242 us
    pallas_call x1, Pallas kernels: 250 us -> 242 us  [shards(): pl.pallas_call(kernel, out_shape=[jax.ShapeDtypeStruct(array.shape, F32)...]
where the time goes in v3:
time: 249 us
  Pallas kernels  242 us (97%)
  other arithmetic  5.12 us (2%)
    pallas_call x1, Pallas kernels, shards(): pl.pallas_call(kernel, out_shape=[jax.ShapeDtypeStruct(array.shape, F32)...  242 us

profile of v3, /device:TPU:6, one launch (start us, length us, event | category | flops | bytes accessed | tf_op | source)
XLA Modules:
  0.0 248.8 jit_solution(7623772875364107182)
XLA Ops:
  0.6 1.4 copy.16.table
  2.0 0.0 copy-start
  2.0 241.6 %shard_map.147 = (f32[8,16,2048]{2,1,0:T(8,128)}, f32[8,64,512]{2,1,0:T(8,128)}) custom-call(s32[64,2]{1,0:T(8,128)} %copy.16.table, s32[1,384]{1,0:T(1,128)} %ids.1, bf16[384,1024]{1,0:T(8,128)(2,1)} %bitcast.10, bf16[384,1024]{1,0:T(8,128)(2,1)} %bitcast.11, f32[8,16,2048]{2,1,0:T(8,128)} %um_in.1, f32[8,64,512]{2,1,0:T(8,128)} %dm_in.1, ...), custom_call_target="tpu_custom_call" | custom-call | flops 12884901888 | bytes 30000000 | tf_op jit(solution)/shard_map/pallas_call | solution.py:502
  243.6 0.0 copy-start.1
  243.6 0.0 copy-start.2
  243.6 0.0 copy-start.3
  243.7 0.0 copy-done
  243.7 3.4 %multiply_subtract_fusion.1 = (f32[8,16,2048]{2,1,0:T(8,128)}, f32[8,16,2048]{2,1,0:T(8,128)}) fusion(f32[8,16,2048]{2,1,0:T(8,128)S(1)} %copy-done, f32[8,16,2048]{2,1,0:T(8,128)} %get-tuple-element.6, f32[8,16,2048]{2,1,0:T(8,128)} %param.18), kind=kLoop, calls=%fused_computation.2 | loop fusion | flops 1572864 | bytes 5242880 | tf_op jit(solution)/shard_map/sub | solution.py:578
  247.1 0.0 copy-done.1
  247.1 0.0 copy-done.2
  247.1 0.0 copy-done.3
  247.1 1.7 multiply_subtract_fusion
Async XLA Ops:
  2.0 241.6 %copy-start = (f32[8,16,2048]{2,1,0:T(8,128)S(1)}, f32[8,16,2048]{2,1,0:T(8,128)}, u32[]{:S(2)}) copy-start(f32[8,16,2048]{2,1,0:T(8,128)} %um_in.1) | copy-start | bytes 3145732
  243.6 3.5 %copy-start.1 = (f32[8,64,512]{2,1,0:T(8,128)S(1)}, f32[8,64,512]{2,1,0:T(8,128)}, u32[]{:S(2)}) copy-start(f32[8,64,512]{2,1,0:T(8,128)} %dm_in.1) | copy-start | bytes 3145732
  243.6 3.5 %copy-start.2 = (f32[8,64,512]{2,1,0:T(8,128)S(1)}, f32[8,64,512]{2,1,0:T(8,128)}, u32[]{:S(2)}) copy-start(f32[8,64,512]{2,1,0:T(8,128)} %param.19) | copy-start | bytes 3145732
  243.6 3.4 %copy-start.3 = (f32[8,64,512]{2,1,0:T(8,128)S(1)}, f32[8,64,512]{2,1,0:T(8,128)}, u32[]{:S(2)}) copy-start(f32[8,64,512]{2,1,0:T(8,128)} %get-tuple-element.7) | copy-start | bytes 3145732

commit v4 on v3

--- a/solution.py
+++ b/solution.py
@@ -32,10 +32,11 @@
 
 def kernel(
     table, ids, act_in, cot_in, um_in, dm_in, up_first, up_second, down_first, down_second, um_out, dm_out,
-    um, dm, act, cot, upb, upf, dnb, blk, buf_a, buf_b, wup, wdn, rdn, rup,
+    um, dm, up_x0, up_x1, up_x2, up_x3, up_z0, up_z1, up_z2, up_z3,
+    dn_x0, dn_x1, dn_x2, dn_x3, dn_z0, dn_z1, dn_z2, dn_z3, dnb, buf_a, buf_b, wup, wdn, rdn, rup,
     gsend, gmine, grecv, nrm, nrm_t, og, count, used, gp, wide_a, act_a, wide_b, mom,
     pdn_send, pdn_recv, pup_send, pup_recv, pick_t, pick_up, pick_dn,
-    in_sem, mom_sem, out_sem, y_send, y_recv, dn_send, blk_recv, wu_send, wu_recv, wd_send, wd_recv,
+    in_sem, mom_sem, out_sem, y_send, y_recv, ring_send, ring_recv, dn_send, blk_recv, wu_send, wu_recv, wd_send, wd_recv,
     g_send, g_recv, dd_send, dd_recv, du_send, du_recv,
 ):
     path = lax.axis_index("path")
@@ -67,10 +68,11 @@
     def settle(ref, sem):
         pltpu.make_async_copy(ref, ref, sem).wait()
 
+    own_rows = pl.ds(pl.multiple_of(here * TOK, TOK), TOK)
     loads = [
         pltpu.make_async_copy(src, dst, in_sem.at[i])
         for i, (src, dst) in enumerate(
-            [(um_in, um), (act_in, act), (dm_in, dm), (cot_in, cot)]
+            [(um_in, um), (act_in, nrm.at[own_rows]), (dm_in, dm), (cot_in, og.at[own_rows])]
         )
     ]
     for load in loads:
@@ -93,71 +95,121 @@
     ):
         pl.semaphore_signal(barrier, inc=1, device_id=(to_path, to_dp), device_id_type=MESH)
 
-    def pick_up_rows(side, source):
+    def ring(row, blocks, minus, plus):
+        own, from_minus, from_plus, opposite = blocks
+        halves = pl.ds(0, C // 2), pl.ds(C // 2, C // 2)
+        hops = [
+            (own, from_minus, plus),
+            (own, from_plus, minus),
+            (from_minus.at[halves[0]], opposite.at[halves[0]], plus),
+            (from_plus.at[halves[1]], opposite.at[halves[1]], minus),
+        ]
+        return [
+            remote(src, dst, ring_send.at[row, n], ring_recv.at[row, n], to, here)
+            for n, (src, dst, to) in enumerate(hops)
+        ]
+
+    x_minus, x_plus = place(lax.rem(x + 3, 4), yl, zc), place(lax.rem(x + 1, 4), yl, zc)
+    z_minus = place(x, yl, lax.rem(z + 3, 4) * 2 + core)
+    z_plus = place(x, yl, lax.rem(z + 1, 4) * 2 + core)
+    up_x, up_z = (up_x0, up_x1, up_x2, up_x3), (up_z0, up_z1, up_z2, up_z3)
+    dn_x, dn_z = (dn_x0, dn_x1, dn_x2, dn_x3), (dn_z0, dn_z1, dn_z2, dn_z3)
+    rings = [
+        ring(0, up_x, x_minus, x_plus),
+        ring(1, up_z, z_minus, z_plus),
+        ring(2, dn_x, x_minus, x_plus),
+        ring(3, dn_z, z_minus, z_plus),
+    ]
+    shift = (0, 3, 1, 2)
+
+    def along_z(k):
+        return x, zc_at(k)
+
+    def along_x(k):
+        return lax.rem(x + lax.div(k, 2), 4), z * 2 + lax.rem(core + k, 2)
+
+    def pick_and_send(level, blocks, part, first_slot, peers, buf, landing, send, recv):
+        def make(k):
+            x_, zc_ = peers(k)
+            slot = first_slot + part * 8 + k
+            buf[slot] = blocks[part][table[place(x_, yl, zc_), level]]
+            return buf.at[slot], place(x_, yl, zc_)
+
+        source, _ = make(0)
+        pltpu.make_async_copy(source, landing, recv).start()
+
         def one(k, _):
-            module = table[lax.div(k, 8) * 16 + yl * 8 + lax.rem(k, 8), 0]
-            buf_a[side * GROUP + k] = source[module]
+            source, to_path = make(k)
+            remote(source, landing, send, recv, to_path, here).start()
             return 0
 
-        lax.fori_loop(0, GROUP, one, 0)
+        lax.fori_loop(1, 8, one, 0)
+
+    def up_picks_x(part):
+        from_x = lax.rem(x + shift[part], 4)
+        pick_and_send(0, up_x, part, 0, along_z, buf_a, wup.at[from_x, yl, zc], wu_send, wu_recv)
+
+    def up_picks_z(part):
+        from_zc = lax.rem(z + shift[part], 4) * 2 + core
+        pick_and_send(0, up_z, part, GROUP, along_x, buf_a, wup.at[x, other_yl, from_zc], wu_send, wu_recv)
+
+    def dn_landing(x_, side, zc_):
+        crossed = lax.rem(lax.div(x_, 2) + here, 2)
+        owner_x = x_ + crossed * (3 - 2 * x_)
+        owner_dp = here + crossed * (1 - 2 * here)
+        return wdn.at[owner_dp, (owner_x - 2 * here) * 16 + side * 8 + zc_]
+
+    def dn_picks_x(part):
+        landing = dn_landing(lax.rem(x + shift[part], 4), 0, zc)
+        pick_and_send(1, dn_x, part, 0, along_z, buf_b, landing, wd_send, wd_recv)
+
+    def dn_picks_z(part):
+        landing = dn_landing(x, 1, lax.rem(z + shift[part], 4) * 2 + core)
+        pick_and_send(1, dn_z, part, GROUP, along_x, buf_b, landing, wd_send, wd_recv)
 
     loads[0].wait()
-    upb[...] = um[...].astype(BF16)
-    pick_up_rows(yl, upb)
+    up_x0[...] = um[...].astype(BF16)
     pl.semaphore_wait(barrier, GROUP + 3)
-
-    up_swap = remote(upb, upf, y_send.at[0], y_recv.at[0], place(x, other_yl, zc), here)
+    up_swap = remote(up_x0, up_z0, y_send.at[0], y_recv.at[0], place(x, other_yl, zc), here)
     up_swap.start()
-
-    def send_up_rows(side, half):
-        row = place(x, side, zc)
-        pltpu.make_async_copy(buf_a.at[side * GROUP + group], wup.at[row], wu_recv).start()
-
-        def one(k, _):
-            x_, zc_ = peer(lax.rem(k * 11, GROUP))
-            remote(
-                buf_a.at[side * GROUP + x_ * 8 + zc_], wup.at[row], wu_send.at[half], wu_recv, place(x_, yl, zc_), here
-            ).start()
-            return 0
-
-        lax.fori_loop(1, GROUP, one, 0)
-
-    send_up_rows(yl, 0)
-
-    own_rows = pl.ds(pl.multiple_of(here * TOK, TOK), TOK)
-    loads[1].wait()
-    for part in range(3):
-        rows = pl.ds(part * 128, 128)
-        wide = act[rows, :].astype(F32)
-        mean_square = jnp.mean(wide * wide, axis=-1, keepdims=True)
-        to_rows = pl.ds(pl.multiple_of(here * TOK + part * 128, 128), 128)
-        nrm[to_rows, :] = (wide * lax.rsqrt(mean_square + 1e-06)).astype(BF16)
-    nrm_swap = remote(nrm.at[own_rows], nrm.at[own_rows], y_send.at[1], y_recv.at[1], path, there)
-    nrm_swap.start()
+    rings[0][0].start()
+    rings[0][1].start()
+    up_picks_x(0)
 
     loads[2].wait()
     dnb[...] = dm[...].astype(BF16)
     x_to = x + cross * (3 - 2 * x)
     dp_to = here + cross * (1 - 2 * here)
-    dn_far = remote(dnb, blk.at[yl], dn_send.at[0], blk_recv, place(x_to, other_yl, zc), dp_to)
-    dn_far.start()
-    dn_near = remote(dnb, blk.at[yl], dn_send.at[1], blk_recv, place(3 - x, yl, zc), there)
-
-    @pl.when(cross == 1)
-    def _():
-        dn_near.start()
-
-    @pl.when(cross == 0)
-    def _():
-        pltpu.make_async_copy(dnb, blk.at[yl], blk_recv).start()
-
+
+    def dn_copies(side):
+        own = (dn_x0, dn_z0)[side]
+        far = remote(dnb, own, dn_send.at[0], blk_recv.at[side], place(x_to, other_yl, zc), dp_to)
+        near = remote(dnb, own, dn_send.at[1], blk_recv.at[side], place(3 - x, yl, zc), there)
+        return far, near, pltpu.make_async_copy(dnb, own, blk_recv.at[side])
+
+    for side in range(2):
+
+        @pl.when(yl == side)
+        def _(side=side):
+            far, near, local = dn_copies(side)
+            far.start()
+            pl.when(cross == 1)(near.start)
+            pl.when(cross == 0)(local.start)
+
+    loads[1].wait()
+    for part in range(3):
+        rows = pl.ds(pl.multiple_of(here * TOK + part * 128, 128), 128)
+        wide = nrm[rows, :].astype(F32)
+        mean_square = jnp.mean(wide * wide, axis=-1, keepdims=True)
+        nrm[rows, :] = (wide * lax.rsqrt(mean_square + 1e-06)).astype(BF16)
+    nrm_swap = remote(nrm.at[own_rows], nrm.at[own_rows], y_send.at[1], y_recv.at[1], path, there)
+    nrm_swap.start()
     loads[3].wait()
     live = jnp.sum((ids[...] != 0).astype(F32))
     for part in range(3):
-        rows = pl.ds(part * 128, 128)
-        to_rows = pl.ds(pl.multiple_of(here * TOK + part * 128, 128), 128)
+        rows = pl.ds(pl.multiple_of(here * TOK + part * 128, 128), 128)
         position = (lax.broadcasted_iota(jnp.int32, (128, D), 0) + part * 128).astype(F32)
-        og[to_rows, :] = jnp.where(position < live, cot[rows, :].astype(F32), 0.0).astype(BF16)
+        og[rows, :] = jnp.where(position < live, og[rows, :].astype(F32), 0.0).astype(BF16)
     count[0] = jnp.broadcast_to(live, (8, 128))
     count_swap = remote(count.at[0], count.at[1], y_send.at[3], y_recv.at[3], path, there)
     count_swap.start()
@@ -165,34 +217,41 @@
     og_swap.start()
 
     up_swap.wait()
-    pick_up_rows(other_yl, upf)
-    send_up_rows(other_yl, 1)
-
-    settle(blk, blk_recv)
-
-    def pick_down_rows(k, _):
-        module = table[lax.div(k, 8) * 16 + yl * 8 + lax.rem(k, 8), 1]
-        buf_b[k] = blk[0, module]
-        buf_b[GROUP + k] = blk[1, module]
-        return 0
-
-    lax.fori_loop(0, GROUP, pick_down_rows, 0)
-
-    settle(buf_a.at[pl.ds(0, GROUP - 1)], wu_send.at[0])
-    from_x = x_to - 2 * here
+    rings[1][0].start()
+    rings[1][1].start()
+    up_picks_z(0)
+
+    def pass_on(row):
+        for n in range(2):
+            rings[row][n].wait_recv()
+            rings[row][n + 2].start()
+
+    def await_opposite(row):
+        for n in range(2, 4):
+            rings[row][n].wait_recv()
+
+    pass_on(0)
+    up_picks_x(1)
+    up_picks_x(2)
     for side in range(2):
-        row = from_x * 16 + side * 8 + zc
-        pltpu.make_async_copy(buf_b.at[side * GROUP + group], wdn.at[dp_to, row], wd_recv).start()
-
-        def one(k, _, side=side, row=row):
-            x_, zc_ = peer(lax.rem(k * 11, GROUP))
-            remote(
-                buf_b.at[side * GROUP + x_ * 8 + zc_], wdn.at[dp_to, row], wd_send, wd_recv,
-                place(x_, yl, zc_), here,
-            ).start()
-            return 0
-
-        lax.fori_loop(1, GROUP, one, 0)
+        dn_copies(side)[0].wait_recv()
+        rings[2 + side][0].start()
+        rings[2 + side][1].start()
+    pass_on(1)
+    up_picks_z(1)
+    up_picks_z(2)
+    await_opposite(0)
+    up_picks_x(3)
+    await_opposite(1)
+    up_picks_z(3)
+    dn_picks_x(0)
+    dn_picks_z(0)
+    pass_on(2)
+    dn_picks_x(1)
+    dn_picks_x(2)
+    pass_on(3)
+    dn_picks_z(1)
+    dn_picks_z(2)
 
     nrm_swap.wait()
 
@@ -215,7 +274,7 @@
     lax.fori_loop(0, 12, scale_rows, 0)
 
     down_x = [here * 2 + lax.rem(x + i, 2) for i in range(2)] + [there * 2 + lax.rem(x + i, 2) for i in range(2)]
-    up_x = [lax.rem(x + i, 4) for i in (2, 1, 3, 0)]
+    up_block = [lax.rem(x + i, 4) for i in (2, 1, 3, 0)]
 
     order = (0, 1, 2, 3, 4, 5, 6, 7)
 
@@ -231,7 +290,7 @@
                     down_source.at[rows], mom.at[slot, kind], mom_sem.at[slot, kind]
                 ).start()
             else:
-                rows = pl.ds(pl.multiple_of(up_x[step - 4] * 256, 256), 256)
+                rows = pl.ds(pl.multiple_of(up_block[step - 4] * 256, 256), 256)
                 for b in range(4):
                     pltpu.make_async_copy(
                         up_source.at[rows, pl.ds(b * 512, 512)],
@@ -257,7 +316,7 @@
 
     def pre_act(i, half):
         cols = pl.ds(pl.multiple_of(i * 256, 256), 256)
-        weights = wup[:, :, cols].reshape(D, 256)
+        weights = wup[:, :, :, :, cols].reshape(D, 256)
         wide_a[half] = jnp.dot(nrm[...], weights, preferred_element_type=F32)
 
     first_tile = 4 * lax.rem(x, 2)
@@ -286,6 +345,11 @@
 
     lax.fori_loop(0, 4, hidden, 0)
 
+    await_opposite(2)
+    dn_picks_x(3)
+    await_opposite(3)
+    dn_picks_z(3)
+
     def down_delta(turn_no):
         step = order[turn_no]
         x_ = down_x[step]
@@ -330,7 +394,7 @@
 
         lax.fori_loop(0, 8, send, 0)
 
-    settle(buf_a.at[pl.ds(0, GROUP - 1)], wu_send.at[1])
+    settle(buf_a.at[pl.ds(0, 2 * GROUP - 8)], wu_send)
     for turn_no in range(4):
         down_delta(turn_no)
         send_down_delta(turn_no, other_yl)
@@ -348,7 +412,7 @@
         return 0
 
     lax.fori_loop(0, 8, hidden_grad, 0)
-    settle(buf_b.at[pl.ds(0, 2 * GROUP - 2)], wd_send)
+    settle(buf_b.at[pl.ds(0, 2 * GROUP - 8)], wd_send)
 
     def send_up_delta(x_, zc_, side):
         row = x_ * 16 + side * 8 + zc_
@@ -365,7 +429,7 @@
             pltpu.make_async_copy(buf_b.at[row], rup.at[side, group], du_recv.at[side]).start()
 
     def up_step(turn_no):
-        x_ = up_x[order[turn_no] - 4]
+        x_ = up_block[order[turn_no] - 4]
         slot = turn_no % 2
         lhs = nrm_t[pl.ds(pl.multiple_of(x_ * 256, 256), 256), :]
 
@@ -467,12 +531,12 @@
         finish(total, um, 0, pl.ds(0, 16), pl.ds(b * 512, 512))
     stores[1].start()
 
-    dn_far.wait_send()
-
-    @pl.when(cross == 1)
-    def _():
-        dn_near.wait_send()
-
+    far, near, _ = dn_copies(0)
+    far.wait_send()
+    pl.when(cross == 1)(near.wait_send)
+    for hops in rings:
+        for hop in hops:
+            hop.wait_send()
     for chunk in range(4):
         g_copy(chunk).wait_send()
     settle(buf_a.at[pl.ds(0, 2 * GROUP - 2)], dd_send)
@@ -507,15 +571,12 @@
         scratch_shapes=[
             pltpu.VMEM((C, 16, HALF_F), F32),
             pltpu.VMEM((C, 64, HALF_D), F32),
-            pltpu.VMEM((TOK, D), BF16),
-            pltpu.VMEM((TOK, D), BF16),
-            pltpu.VMEM((C, 16, HALF_F), BF16),
-            pltpu.VMEM((C, 16, HALF_F), BF16),
+            *[pltpu.VMEM((C, 16, HALF_F), BF16)] * 8,
+            *[pltpu.VMEM((C, 64, HALF_D), BF16)] * 8,
             pltpu.VMEM((C, 64, HALF_D), BF16),
-            pltpu.VMEM((2, C, 64, HALF_D), BF16),
             pltpu.VMEM((2 * GROUP, 16, HALF_F), BF16),
             pltpu.VMEM((2 * GROUP, 64, HALF_D), BF16),
-            pltpu.VMEM((2 * GROUP, 16, HALF_F), BF16),
+            pltpu.VMEM((4, 2, 8, 16, HALF_F), BF16),
             pltpu.VMEM((2, GROUP, 64, HALF_D), BF16),
             pltpu.VMEM((2, GROUP, 16, HALF_F), BF16),
             pltpu.VMEM((2, GROUP, 64, HALF_D), BF16),
@@ -544,9 +605,11 @@
             dma((2,)),
             dma((6,)),
             dma((6,)),
+            dma((4, 4)),
+            dma((4, 4)),
+            dma((2,)),
             dma((2,)),
             dma,
-            dma((2,)),
             dma,
             dma,
             dma,

time: 249 us -> 255 us (1.024)
  the two profiles are of different devices: /device:TPU:6 before, /device:TPU:61 now
where the time goes in v4:
time: 255 us; the launch traced here: 254 us
  Pallas kernels  247 us (97%)
  other arithmetic  5.12 us (2%)
    pallas_call x1, Pallas kernels, shards(): pl.pallas_call(kernel, out_shape=[jax.ShapeDtypeStruct(array.shape, F32)...  247 us

profile of v4, /device:TPU:61, one launch (start us, length us, event | category | flops | bytes accessed | tf_op | source)
XLA Modules:
  0.0 254.5 jit_solution(7993119485288809385)
XLA Ops:
  0.6 1.4 copy.16.table
  2.0 0.0 copy-start
  2.0 247.3 %shard_map.147 = (f32[8,16,2048]{2,1,0:T(8,128)}, f32[8,64,512]{2,1,0:T(8,128)}) custom-call(s32[64,2]{1,0:T(8,128)} %copy.16.table, s32[1,384]{1,0:T(1,128)} %ids.1, bf16[384,1024]{1,0:T(8,128)(2,1)} %bitcast.10, bf16[384,1024]{1,0:T(8,128)(2,1)} %bitcast.11, f32[8,16,2048]{2,1,0:T(8,128)} %um_in.1, f32[8,64,512]{2,1,0:T(8,128)} %dm_in.1, ...), custom_call_target="tpu_custom_call" | custom-call | flops 12884901888 | bytes 30000000 | tf_op jit(solution)/shard_map/pallas_call | solution.py:566
  249.3 0.0 copy-start.1
  249.3 0.0 copy-start.2
  249.3 0.0 copy-start.3
  249.3 0.0 copy-done
  249.4 3.4 %multiply_subtract_fusion.1 = (f32[8,16,2048]{2,1,0:T(8,128)}, f32[8,16,2048]{2,1,0:T(8,128)}) fusion(f32[8,16,2048]{2,1,0:T(8,128)S(1)} %copy-done, f32[8,16,2048]{2,1,0:T(8,128)} %get-tuple-element.6, f32[8,16,2048]{2,1,0:T(8,128)} %param.18), kind=kLoop, calls=%fused_computation.2 | loop fusion | flops 1572864 | bytes 5242880 | tf_op jit(solution)/shard_map/sub | solution.py:641
  252.8 0.0 copy-done.1
  252.8 0.0 copy-done.2
  252.8 0.0 copy-done.3
  252.8 1.7 multiply_subtract_fusion
Async XLA Ops:
  2.0 247.3 %copy-start = (f32[8,16,2048]{2,1,0:T(8,128)S(1)}, f32[8,16,2048]{2,1,0:T(8,128)}, u32[]{:S(2)}) copy-start(f32[8,16,2048]{2,1,0:T(8,128)} %um_in.1) | copy-start | bytes 3145732
  249.3 3.5 %copy-start.1 = (f32[8,64,512]{2,1,0:T(8,128)S(1)}, f32[8,64,512]{2,1,0:T(8,128)}, u32[]{:S(2)}) copy-start(f32[8,64,512]{2,1,0:T(8,128)} %dm_in.1) | copy-start | bytes 3145732
  249.3 3.5 %copy-start.2 = (f32[8,64,512]{2,1,0:T(8,128)S(1)}, f32[8,64,512]{2,1,0:T(8,128)}, u32[]{:S(2)}) copy-start(f32[8,64,512]{2,1,0:T(8,128)} %param.19) | copy-start | bytes 3145732
  249.3 3.4 %copy-start.3 = (f32[8,64,512]{2,1,0:T(8,128)S(1)}, f32[8,64,512]{2,1,0:T(8,128)}, u32[]{:S(2)}) copy-start(f32[8,64,512]{2,1,0:T(8,128)} %get-tuple-element.7) | copy-start | bytes 3145732

commit v5 on v4

--- a/solution.py
+++ b/solution.py
@@ -273,10 +273,10 @@
 
     lax.fori_loop(0, 12, scale_rows, 0)
 
-    down_x = [here * 2 + lax.rem(x + i, 2) for i in range(2)] + [there * 2 + lax.rem(x + i, 2) for i in range(2)]
+    down_x = [half * 2 + lax.rem(x + i, 2) for half in (here, there) for i in range(2)]
     up_block = [lax.rem(x + i, 4) for i in (2, 1, 3, 0)]
 
-    order = (0, 1, 2, 3, 4, 5, 6, 7)
+    order = (0, 1, 2, 4, 5, 6, 7, 3)
 
     def fetch(turn_no):
         if turn_no >= 8:
@@ -395,10 +395,11 @@
         lax.fori_loop(0, 8, send, 0)
 
     settle(buf_a.at[pl.ds(0, 2 * GROUP - 8)], wu_send)
-    for turn_no in range(4):
+    for turn_no in range(3):
         down_delta(turn_no)
-        send_down_delta(turn_no, other_yl)
-        send_down_delta(turn_no, yl)
+        if turn_no != 1:
+            send_down_delta(order[turn_no], other_yl)
+            send_down_delta(order[turn_no], yl)
 
     settle(wdn, wd_recv)
 
@@ -454,7 +455,7 @@
 
         lax.fori_loop(0, 8, send, 0)
 
-    for turn_no in range(4, 8):
+    for turn_no in range(3, 7):
         up_step(turn_no)
 
     def send_rest(k, _):
@@ -463,6 +464,10 @@
         return 0
 
     lax.fori_loop(0, GROUP, send_rest, 0)
+    down_delta(7)
+    for side in (other_yl, yl):
+        send_down_delta(1, side)
+        send_down_delta(3, side)
 
     lane = lax.broadcasted_iota(jnp.int32, (16, C * 16), 1)
     same_row = (lane & 15) == lax.broadcasted_iota(jnp.int32, (16, C * 16), 0)
@@ -505,6 +510,19 @@
     stores = [
         pltpu.make_async_copy(src, dst, out_sem.at[i]) for i, (src, dst) in enumerate([(dm, dm_out), (um, um_out)])
     ]
+    settle(rup.at[other_yl], du_recv.at[other_yl])
+    for b in range(4):
+        pup_send[:, pl.ds(b * 16, 16), :] = up_sum(other_yl, b).astype(BF16)
+    up_part = remote(pup_send, pup_recv, y_send.at[5], y_recv.at[5], mate, here)
+    up_part.start()
+    settle(rup.at[yl], du_recv.at[yl])
+    up_part.wait()
+    for b in range(4):
+        rows = pl.ds(b * 16, 16)
+        total = up_sum(yl, b) + pup_recv[:, rows, :].astype(F32)
+        finish(total, um, 0, pl.ds(0, 16), pl.ds(b * 512, 512))
+    stores[1].start()
+
     settle(rdn.at[other_yl], dd_recv.at[other_yl])
     for b in range(4):
         pdn_send[:, :, pl.ds(b * 512, 512)] = down_sum(other_yl, b).astype(BF16)
@@ -517,19 +535,6 @@
         total = down_sum(yl, b) + pdn_recv[:, :, cols].astype(F32)
         finish(total, dm, 1, pl.ds(b * 16, 16), pl.ds(0, 512))
     stores[0].start()
-
-    settle(rup.at[other_yl], du_recv.at[other_yl])
-    for b in range(4):
-        pup_send[:, pl.ds(b * 16, 16), :] = up_sum(other_yl, b).astype(BF16)
-    up_part = remote(pup_send, pup_recv, y_send.at[5], y_recv.at[5], mate, here)
-    up_part.start()
-    settle(rup.at[yl], du_recv.at[yl])
-    up_part.wait()
-    for b in range(4):
-        rows = pl.ds(b * 16, 16)
-        total = up_sum(yl, b) + pup_recv[:, rows, :].astype(F32)
-        finish(total, um, 0, pl.ds(0, 16), pl.ds(b * 512, 512))
-    stores[1].start()
 
     far, near, _ = dn_copies(0)
     far.wait_send()

time: 255 us -> 250 us (0.980)
  the two profiles are of different devices: /device:TPU:61 before, /device:TPU:18 now
where the time goes in v5:
time: 250 us
  Pallas kernels  243 us (97%)
  other arithmetic  5.12 us (2%)
    pallas_call x1, Pallas kernels, shards(): pl.pallas_call(kernel, out_shape=[jax.ShapeDtypeStruct(array.shape, F32)...  243 us

profile of v5, /device:TPU:18, one launch (start us, length us, event | category | flops | bytes accessed | tf_op | source)
XLA Modules:
  0.0 249.7 jit_solution(11022226607983057535)
XLA Ops:
  0.6 1.4 copy.16.table
  2.0 0.0 copy-start
  2.0 242.5 %shard_map.147 = (f32[8,16,2048]{2,1,0:T(8,128)}, f32[8,64,512]{2,1,0:T(8,128)}) custom-call(s32[64,2]{1,0:T(8,128)} %copy.16.table, s32[1,384]{1,0:T(1,128)} %ids.1, bf16[384,1024]{1,0:T(8,128)(2,1)} %bitcast.10, bf16[384,1024]{1,0:T(8,128)(2,1)} %bitcast.11, f32[8,16,2048]{2,1,0:T(8,128)} %um_in.1, f32[8,64,512]{2,1,0:T(8,128)} %dm_in.1, ...), custom_call_target="tpu_custom_call" | custom-call | flops 12884901888 | bytes 30000000 | tf_op jit(solution)/shard_map/pallas_call | solution.py:571
  244.6 0.0 copy-start.1
  244.6 0.0 copy-start.2
  244.6 0.0 copy-start.3
  244.6 0.0 copy-done
  244.6 3.4 %multiply_subtract_fusion.1 = (f32[8,16,2048]{2,1,0:T(8,128)}, f32[8,16,2048]{2,1,0:T(8,128)}) fusion(f32[8,16,2048]{2,1,0:T(8,128)S(1)} %copy-done, f32[8,16,2048]{2,1,0:T(8,128)} %get-tuple-element.6, f32[8,16,2048]{2,1,0:T(8,128)} %param.18), kind=kLoop, calls=%fused_computation.2 | loop fusion | flops 1572864 | bytes 5242880 | tf_op jit(solution)/shard_map/sub | solution.py:646
  248.0 0.0 copy-done.1
  248.0 0.0 copy-done.2
  248.0 0.0 copy-done.3
  248.0 1.7 multiply_subtract_fusion
Async XLA Ops:
  2.0 242.6 %copy-start = (f32[8,16,2048]{2,1,0:T(8,128)S(1)}, f32[8,16,2048]{2,1,0:T(8,128)}, u32[]{:S(2)}) copy-start(f32[8,16,2048]{2,1,0:T(8,128)} %um_in.1) | copy-start | bytes 3145732
  244.6 3.5 %copy-start.1 = (f32[8,64,512]{2,1,0:T(8,128)S(1)}, f32[8,64,512]{2,1,0:T(8,128)}, u32[]{:S(2)}) copy-start(f32[8,64,512]{2,1,0:T(8,128)} %dm_in.1) | copy-start | bytes 3145732
  244.6 3.5 %copy-start.2 = (f32[8,64,512]{2,1,0:T(8,128)S(1)}, f32[8,64,512]{2,1,0:T(8,128)}, u32[]{:S(2)}) copy-start(f32[8,64,512]{2,1,0:T(8,128)} %param.19) | copy-start | bytes 3145732
  244.6 3.4 %copy-start.3 = (f32[8,64,512]{2,1,0:T(8,128)S(1)}, f32[8,64,512]{2,1,0:T(8,128)}, u32[]{:S(2)}) copy-start(f32[8,64,512]{2,1,0:T(8,128)} %get-tuple-element.7) | copy-start | bytes 3145732

commit v6 on v5

v6 whole, which is shorter than its diff:
```python
import jax
import jax.numpy as jnp
from jax import lax
from jax.experimental import pallas as pl
from jax.experimental.pallas import tpu as pltpu
from jax.sharding import PartitionSpec as P

D = 1024
F = 4096
C = 8
TOK = 384
HALF_F = F // 2
HALF_D = D // 2
GROUP = 32
MESH = pl.DeviceIdType.MESH
BF16 = jnp.bfloat16
F32 = jnp.float32
NT = (((1,), (1,)), ((), ()))
TN = (((0,), (0,)), ((), ()))
UP_SCALE = D ** (-0.5)
DOWN_SCALE = F ** (-0.5)


def step_direction(gradient, first_moment, second_moment):
    first_new = 0.9 * first_moment.astype(F32) + 0.1 * gradient
    second_new = 0.95 * second_moment.astype(F32) + 0.05 * gradient * gradient
    below = second_new * lax.rsqrt(second_new) + 1e-08
    over = pl.reciprocal(below, approx=True)
    over = over * (2.0 - below * over)
    return (0.1 * first_new * over).astype(BF16)


def kernel(
    table, ids, act_in, cot_in, um_in, dm_in, up_first, up_second, down_first, down_second, um_out, dm_out,
    um, dm, up_x0, up_x1, up_x2, up_x3, up_z0, up_z1, up_z2, up_z3,
    dn_x0, dn_x1, dn_x2, dn_x3, dn_z0, dn_z1, dn_z2, dn_z3, dnb, buf_a, buf_b, wup, wdn, rdn, rup,
    gsend, gmine, grecv, nrm, nrm_t, og, count, used, gp, wide_a, act_a, wide_b, mom,
    pdn_send, pdn_recv, pup_send, pup_recv, pick_t, pick_up, pick_dn,
    in_sem, mom_sem, out_sem, y_send, y_recv, ring_send, ring_recv, dn_send, blk_recv, wu_send, wu_recv, wd_send, wd_recv,
    g_send, g_recv, dd_send, dd_recv, du_send, du_recv,
):
    path = lax.axis_index("path")
    here = lax.axis_index("dp")
    x = lax.div(path, 16)
    yl = lax.rem(lax.div(path, 8), 2)
    zc = lax.rem(path, 8)
    z = lax.div(zc, 2)
    core = lax.rem(zc, 2)
    group = x * 8 + zc
    other_yl = 1 - yl
    there = 1 - here

    def place(x_, yl_, zc_):
        return x_ * 16 + yl_ * 8 + zc_

    def zc_at(k):
        return lax.rem(z + lax.rem(lax.div(k, 2), 4), 4) * 2 + lax.rem(core + k, 2)

    def peer(k):
        return lax.rem(x + lax.div(k, 8), 4), zc_at(k)

    def remote(src, dst, send, recv, to_path, to_dp):
        return pltpu.make_async_remote_copy(
            src_ref=src, dst_ref=dst, send_sem=send, recv_sem=recv,
            device_id=(to_path, to_dp), device_id_type=MESH,
        )

    def settle(ref, sem):
        pltpu.make_async_copy(ref, ref, sem).wait()

    own_rows = pl.ds(pl.multiple_of(here * TOK, TOK), TOK)
    loads = [
        pltpu.make_async_copy(src, dst, in_sem.at[i])
        for i, (src, dst) in enumerate(
            [(um_in, um), (act_in, nrm.at[own_rows]), (dm_in, dm), (cot_in, og.at[own_rows])]
        )
    ]
    for load in loads:
        load.start()

    down_x = [half * 2 + lax.rem(x + i, 2) for half in (here, there) for i in range(2)]
    up_block = [lax.rem(x + (2 + 3 * i) % 4, 4) for i in range(4)]

    order = (0, 1, 4, 5, 2, 6, 7, 3)

    def fetch(turn_no):
        if turn_no >= 8:
            return
        slot = turn_no % 3
        step = order[turn_no]
        for kind, (down_source, up_source) in enumerate(((down_first, up_first), (down_second, up_second))):
            if step < 4:
                rows = pl.ds(pl.multiple_of(down_x[step] * 1024, 1024), 1024)
                pltpu.make_async_copy(
                    down_source.at[rows], mom.at[slot, kind], mom_sem.at[slot, kind]
                ).start()
            else:
                rows = pl.ds(pl.multiple_of(up_block[step - 4] * 256, 256), 256)
                for b in range(4):
                    pltpu.make_async_copy(
                        up_source.at[rows, pl.ds(b * 512, 512)],
                        mom.at[slot, kind, pl.ds(b * 256, 256)],
                        mom_sem.at[slot, kind],
                    ).start()

    def await_moments(slot):
        for kind in range(2):
            settle(mom.at[slot, kind], mom_sem.at[slot, kind])

    for turn_no in range(3):
        fetch(turn_no)

    cross = lax.rem(lax.div(x, 2) + here, 2)
    barrier = pltpu.get_barrier_semaphore()

    def greet(k, _):
        x_, zc_ = peer(k)
        pl.semaphore_signal(barrier, inc=1, device_id=(place(x_, yl, zc_), here), device_id_type=MESH)
        return 0

    lax.fori_loop(1, GROUP, greet, 0)
    for to_path, to_dp in (
        (place(x, other_yl, zc), here),
        (path, there),
        (place(3 - x, yl, zc), there),
        (place(3 - x, other_yl, zc), there),
    ):
        pl.semaphore_signal(barrier, inc=1, device_id=(to_path, to_dp), device_id_type=MESH)

    loads[1].wait()
    for part in range(3):
        rows = pl.ds(pl.multiple_of(here * TOK + part * 128, 128), 128)
        wide = nrm[rows, :].astype(F32)
        mean_square = jnp.mean(wide * wide, axis=-1, keepdims=True)
        nrm[rows, :] = (wide * lax.rsqrt(mean_square + 1e-06)).astype(BF16)
    loads[0].wait()
    up_x0[...] = um[...].astype(BF16)
    loads[3].wait()
    live = jnp.sum((ids[...] != 0).astype(F32))
    for part in range(3):
        rows = pl.ds(pl.multiple_of(here * TOK + part * 128, 128), 128)
        position = (lax.broadcasted_iota(jnp.int32, (128, D), 0) + part * 128).astype(F32)
        og[rows, :] = jnp.where(position < live, og[rows, :].astype(F32), 0.0).astype(BF16)
    count[0] = jnp.broadcast_to(live, (8, 128))
    loads[2].wait()
    dnb[...] = dm[...].astype(BF16)

    def ring(row, blocks, minus, plus):
        own, from_minus, from_plus, opposite = blocks
        halves = pl.ds(0, C // 2), pl.ds(C // 2, C // 2)
        hops = [
            (own, from_minus, plus),
            (own, from_plus, minus),
            (from_minus.at[halves[0]], opposite.at[halves[0]], plus),
            (from_plus.at[halves[1]], opposite.at[halves[1]], minus),
        ]
        return [
            remote(src, dst, ring_send.at[row, n], ring_recv.at[row, n], to, here)
            for n, (src, dst, to) in enumerate(hops)
        ]

    x_minus, x_plus = place(lax.rem(x + 3, 4), yl, zc), place(lax.rem(x + 1, 4), yl, zc)
    z_minus = place(x, yl, lax.rem(z + 3, 4) * 2 + core)
    z_plus = place(x, yl, lax.rem(z + 1, 4) * 2 + core)
    up_x, up_z = (up_x0, up_x1, up_x2, up_x3), (up_z0, up_z1, up_z2, up_z3)
    dn_x, dn_z = (dn_x0, dn_x1, dn_x2, dn_x3), (dn_z0, dn_z1, dn_z2, dn_z3)
    rings = [
        ring(0, up_x, x_minus, x_plus),
        ring(1, up_z, z_minus, z_plus),
        ring(2, dn_x, x_minus, x_plus),
        ring(3, dn_z, z_minus, z_plus),
    ]
    shift = (0, 3, 1, 2)

    def along_z(k):
        return x, zc_at(k)

    def along_x(k):
        return lax.rem(x + lax.div(k, 2), 4), z * 2 + lax.rem(core + k, 2)

    def pick_and_send(level, blocks, part, first_slot, peers, buf, landing, send, recv):
        def make(k):
            x_, zc_ = peers(k)
            slot = first_slot + part * 8 + k
            buf[slot] = blocks[part][table[place(x_, yl, zc_), level]]
            return buf.at[slot], place(x_, yl, zc_)

        source, _ = make(0)
        pltpu.make_async_copy(source, landing, recv).start()

        def one(k, _):
            source, to_path = make(k)
            remote(source, landing, send, recv, to_path, here).start()
            return 0

        lax.fori_loop(1, 8, one, 0)

    def up_picks_x(part):
        from_x = lax.rem(x + shift[part], 4)
        pick_and_send(0, up_x, part, 0, along_z, buf_a, wup.at[from_x, yl, zc], wu_send, wu_recv)

    def up_picks_z(part):
        from_zc = lax.rem(z + shift[part], 4) * 2 + core
        pick_and_send(0, up_z, part, GROUP, along_x, buf_a, wup.at[x, other_yl, from_zc], wu_send, wu_recv)

    def dn_landing(x_, side, zc_):
        crossed = lax.rem(lax.div(x_, 2) + here, 2)
        owner_x = x_ + crossed * (3 - 2 * x_)
        owner_dp = here + crossed * (1 - 2 * here)
        return wdn.at[owner_dp, (owner_x - 2 * here) * 16 + side * 8 + zc_]

    def dn_picks_x(part):
        landing = dn_landing(lax.rem(x + shift[part], 4), 0, zc)
        pick_and_send(1, dn_x, part, 0, along_z, buf_b, landing, wd_send, wd_recv)

    def dn_picks_z(part):
        landing = dn_landing(x, 1, lax.rem(z + shift[part], 4) * 2 + core)
        pick_and_send(1, dn_z, part, GROUP, along_x, buf_b, landing, wd_send, wd_recv)

    pl.semaphore_wait(barrier, GROUP + 3)
    up_swap = remote(up_x0, up_z0, y_send.at[0], y_recv.at[0], place(x, other_yl, zc), here)
    up_swap.start()
    count_swap = remote(count.at[0], count.at[1], y_send.at[3], y_recv.at[3], path, there)
    count_swap.start()
    x_to = x + cross * (3 - 2 * x)
    dp_to = here + cross * (1 - 2 * here)

    def dn_copies(side):
        own = (dn_x0, dn_z0)[side]
        far = remote(dnb, own, dn_send.at[0], blk_recv.at[side], place(x_to, other_yl, zc), dp_to)
        near = remote(dnb, own, dn_send.at[1], blk_recv.at[side], place(3 - x, yl, zc), there)
        return far, near, pltpu.make_async_copy(dnb, own, blk_recv.at[side])

    for side in range(2):

        @pl.when(yl == side)
        def _(side=side):
            far, near, local = dn_copies(side)
            far.start()
            pl.when(cross == 1)(near.start)
            pl.when(cross == 0)(local.start)

    nrm_swap = remote(nrm.at[own_rows], nrm.at[own_rows], y_send.at[1], y_recv.at[1], path, there)
    nrm_swap.start()
    og_swap = remote(og.at[own_rows], og.at[own_rows], y_send.at[2], y_recv.at[2], path, there)
    og_swap.start()

    def pass_on(row):
        for n in range(2):
            rings[row][n].wait_recv()
            rings[row][n + 2].start()

    def await_opposite(row):
        for n in range(2, 4):
            rings[row][n].wait_recv()

    rings[0][0].start()
    rings[0][1].start()
    up_picks_x(0)
    pass_on(0)
    up_picks_x(1)
    up_picks_x(2)
    up_swap.wait()
    rings[1][0].start()
    rings[1][1].start()
    up_picks_z(0)
    await_opposite(0)
    up_picks_x(3)
    pass_on(1)
    up_picks_z(1)
    up_picks_z(2)
    await_opposite(1)
    up_picks_z(3)
    for side in range(2):
        dn_copies(side)[0].wait_recv()
        rings[2 + side][0].start()
        rings[2 + side][1].start()
    dn_picks_x(0)
    dn_picks_z(0)
    pass_on(2)
    pass_on(3)
    dn_picks_x(1)
    dn_picks_z(1)
    dn_picks_x(2)
    dn_picks_z(2)
    await_opposite(2)
    dn_picks_x(3)
    await_opposite(3)
    dn_picks_z(3)

    lane = lax.broadcasted_iota(jnp.int32, (16, C * 16), 1)
    same_row = (lane & 15) == lax.broadcasted_iota(jnp.int32, (16, C * 16), 0)
    for level, pick in enumerate((pick_up, pick_dn)):

        def fill(k, _, level=level):
            module = table[lax.div(k, 8) * 16 + yl * 8 + lax.rem(k, 8), level]
            rows = pl.ds(pl.multiple_of(k * 16, 16), 16)
            pick_t[rows, :] = jnp.where(same_row & ((lane >> 4) == module), 1.0, 0.0)
            return 0

        lax.fori_loop(0, GROUP, fill, 0)
        pick[...] = pick_t[...].T.astype(BF16)

        def tally(k, counts, level=level):
            module = table[k, level]
            return tuple(n + jnp.where(module == m, 1, 0) for m, n in enumerate(counts))

        counts = lax.fori_loop(0, 64, tally, (jnp.int32(0),) * C)
        for m in range(C):
            used[level * C + m] = counts[m]

    nrm_swap.wait()

    def turn(i, _):
        cols = pl.ds(pl.multiple_of(i * 256, 256), 256)
        nrm_t[cols, :] = nrm[:, cols].T
        return 0

    lax.fori_loop(0, 4, turn, 0)
    count_swap.wait()
    per_count = 1.0 / (count[0] + count[1])
    per_count = per_count[0:1, 0:1]
    og_swap.wait()

    def scale_rows(i, _):
        rows = pl.ds(pl.multiple_of(i * 64, 64), 64)
        og[rows, :] = (og[rows, :].astype(F32) * per_count).astype(BF16)
        return 0

    lax.fori_loop(0, 12, scale_rows, 0)

    settle(wup, wu_recv)
    mine_cols = pl.ds(pl.multiple_of(here * HALF_D, HALF_D), HALF_D)
    their_cols = pl.ds(pl.multiple_of(there * HALF_D, HALF_D), HALF_D)

    def g_copy(chunk):
        rows = pl.ds(pl.multiple_of(chunk * 512, 512), 512)
        return remote(gsend.at[rows], grecv.at[rows], g_send.at[chunk], g_recv.at[chunk], path, there)

    def pre_act(i, half):
        cols = pl.ds(pl.multiple_of(i * 256, 256), 256)
        weights = wup[:, :, :, :, cols].reshape(D, 256)
        wide_a[half] = jnp.dot(nrm[...], weights, preferred_element_type=F32)

    first_tile = 4 * lax.rem(x, 2)
    pre_act(first_tile, 0)

    def hidden(pair, _):
        for half in range(2):
            i = lax.rem(first_tile + pair * 2 + half, 8)
            pre_act(lax.rem(i + 1, 8), 1 - half)
            cols = pl.ds(pl.multiple_of(i * 256, 256), 256)
            for strip in range(24):
                rows = pl.ds(strip * 32, 32)
                pre = wide_a[half, rows, :] * UP_SCALE
                sig = 0.5 * jnp.tanh(0.5 * pre) + 0.5
                out = pre * sig
                act_a[half, rows, :] = out.astype(BF16)
                gp[rows, cols] = (sig + out * (1.0 - sig)).astype(BF16)
            out_t = act_a[half].T
            theirs = jnp.dot(out_t, og[:, their_cols], preferred_element_type=F32)
            gsend[cols, :] = (theirs * DOWN_SCALE).astype(BF16)
            if half == 1:
                g_copy(lax.div(i, 2)).start()
            mine = jnp.dot(out_t, og[:, mine_cols], preferred_element_type=F32)
            gmine[cols, :] = (mine * DOWN_SCALE).astype(BF16)
        return 0

    lax.fori_loop(0, 4, hidden, 0)

    def down_delta(turn_no):
        step = order[turn_no]
        x_ = down_x[step]
        source = gmine if step < 2 else grecv
        first_row = lax.rem(x_, 2) * 1024
        if step >= 2:
            for half in range(2):
                g_copy(lax.rem(x_, 2) * 2 + half).wait_recv()
        slot = turn_no % 3
        await_moments(slot)

        def one(q, _):
            for b in range(4):
                rows = pl.ds(pl.multiple_of(q * 64 + b * 16, 16), 16)
                grad = source[pl.ds(pl.multiple_of(first_row + q * 64 + b * 16, 16), 16), :].astype(F32)
                delta = step_direction(grad, mom[slot, 0, rows, :], mom[slot, 1, rows, :])
                buf_a[x_ * 16 + q, :, pl.ds(b * 512, 512)] = delta
            return 0

        lax.fori_loop(0, 16, one, 0)
        fetch(turn_no + 3)

    def send_down_delta(step, side):
        x_ = down_x[step]

        def send(k, _):
            zc_ = zc_at(k)
            row = x_ * 16 + side * 8 + zc_
            away = (x_ * 8 + zc_) != group

            @pl.when(away)
            def _():
                remote(
                    buf_a.at[row], rdn.at[side, group], dd_send, dd_recv.at[side], place(x_, yl, zc_), here
                ).start()

            @pl.when(jnp.logical_not(away))
            def _():
                pltpu.make_async_copy(buf_a.at[row], rdn.at[side, group], dd_recv.at[side]).start()

            return 0

        lax.fori_loop(0, 8, send, 0)

    settle(buf_a.at[pl.ds(0, 2 * GROUP - 8)], wu_send)
    down_delta(0)
    send_down_delta(0, other_yl)
    send_down_delta(0, yl)
    down_delta(1)

    settle(wdn, wd_recv)

    def hidden_grad(i, _):
        cols = pl.ds(pl.multiple_of(i * 256, 256), 256)
        low = wdn[0, pl.ds(i * 4, 4)].reshape(256, HALF_D)
        high = wdn[1, pl.ds(i * 4, 4)].reshape(256, HALF_D)
        grad = lax.dot_general(og[:, pl.ds(0, HALF_D)], low, NT, preferred_element_type=F32)
        grad += lax.dot_general(og[:, pl.ds(HALF_D, HALF_D)], high, NT, preferred_element_type=F32)
        gp[:, cols] = (grad * DOWN_SCALE * gp[:, cols].astype(F32)).astype(BF16)
        return 0

    lax.fori_loop(0, 8, hidden_grad, 0)
    settle(buf_b.at[pl.ds(0, 2 * GROUP - 8)], wd_send)

    def send_up_delta(x_, zc_, side):
        row = x_ * 16 + side * 8 + zc_
        away = (x_ * 8 + zc_) != group

        @pl.when(away)
        def _():
            remote(
                buf_b.at[row], rup.at[side, group], du_send, du_recv.at[side], place(x_, yl, zc_), here
            ).start()

        @pl.when(jnp.logical_not(away))
        def _():
            pltpu.make_async_copy(buf_b.at[row], rup.at[side, group], du_recv.at[side]).start()

    def up_step(step, even):
        x_ = lax.rem(x + lax.rem(2 + 3 * step, 4), 4)
        slot = lax.rem(2 + even, 3)
        lhs = nrm_t[pl.ds(pl.multiple_of(x_ * 256, 256), 256), :]
        await_moments(slot)

        def up_grad(b, half):
            cols = pl.ds(pl.multiple_of(b * 512, 512), 512)
            wide_b[half] = jnp.dot(lhs, gp[:, cols], preferred_element_type=F32)

        def strips(b, half):
            for i in range(16):
                rows = pl.ds(pl.multiple_of(b * 256 + i * 16, 16), 16)
                grad = wide_b[half, pl.ds(i * 16, 16), :] * UP_SCALE
                delta = step_direction(grad, mom[slot, 0, rows, :], mom[slot, 1, rows, :])
                buf_b[x_ * 16 + i, pl.ds(pl.multiple_of(b * 16, 16), 16), :] = delta

        up_grad(0, 0)

        def pair(n, _):
            up_grad(2 * n + 1, 1)
            strips(2 * n, 0)
            up_grad(lax.rem(2 * n + 2, 4), 0)
            strips(2 * n + 1, 1)
            return 0

        lax.fori_loop(0, 2, pair, 0)

        def send(k, _):
            send_up_delta(x_, zc_at(k), lax.rem(other_yl + lax.div(k, 8), 2))
            return 0

        lax.fori_loop(0, 16, send, 0)

    def early(n, _):
        up_step(n, n)
        pl.when(n == 0)(lambda: fetch(5))
        pl.when(n == 1)(lambda: fetch(6))
        return 0

    def late(n, _):
        up_step(n + 2, n)
        return 0

    lax.fori_loop(0, 2, early, 0)
    down_delta(4)
    send_down_delta(2, other_yl)
    send_down_delta(2, yl)
    lax.fori_loop(0, 2, late, 0)
    down_delta(7)
    for side in (other_yl, yl):
        send_down_delta(1, side)
        send_down_delta(3, side)

    def wide_cols(b):
        return pl.ds(pl.multiple_of(b * 512, 512), 512)

    def row_block(b):
        return pl.ds(pl.multiple_of(b * 16, 16), 16)

    def down_sum(side, b):
        block = rdn[side, :, :, wide_cols(b)].reshape(GROUP * 16, 512)
        return jnp.dot(pick_dn[...], block, preferred_element_type=F32).reshape(C, 16, 512)

    def up_sum(side, b):
        block = rup[side, :, row_block(b), :].reshape(GROUP * 16, 512)
        return jnp.dot(pick_up[...], block, preferred_element_type=F32).reshape(C, 16, 512)

    def four(body):
        def one(b, _):
            body(b)
            return 0

        lax.fori_loop(0, 4, one, 0)

    def finish(total, master, level, rows, cols):
        for m in range(C):
            number = jnp.broadcast_to(used[level * C + m].astype(F32), (8, 128))
            per_used = (1.0 / jnp.maximum(number, 1.0))[0:1, 0:1]
            decay = (0.01 * jnp.minimum(number, 1.0))[0:1, 0:1]
            weights = master[m, rows, cols].astype(BF16).astype(F32)
            master[m, rows, cols] = total[m] * per_used + decay * weights

    mate = place(x, other_yl, zc)
    stores = [
        pltpu.make_async_copy(src, dst, out_sem.at[i]) for i, (src, dst) in enumerate([(dm, dm_out), (um, um_out)])
    ]
    settle(rup.at[other_yl], du_recv.at[other_yl])

    @four
    def _(b):
        pup_send[:, row_block(b), :] = up_sum(other_yl, b).astype(BF16)

    up_part = remote(pup_send, pup_recv, y_send.at[5], y_recv.at[5], mate, here)
    up_part.start()
    settle(rup.at[yl], du_recv.at[yl])
    up_part.wait()

    @four
    def _(b):
        total = up_sum(yl, b) + pup_recv[:, row_block(b), :].astype(F32)
        finish(total, um, 0, pl.ds(0, 16), wide_cols(b))

    stores[1].start()

    settle(rdn.at[other_yl], dd_recv.at[other_yl])

    @four
    def _(b):
        pdn_send[:, :, wide_cols(b)] = down_sum(other_yl, b).astype(BF16)

    dn_part = remote(pdn_send, pdn_recv, y_send.at[4], y_recv.at[4], mate, here)
    dn_part.start()
    settle(rdn.at[yl], dd_recv.at[yl])
    dn_part.wait()

    @four
    def _(b):
        total = down_sum(yl, b) + pdn_recv[:, :, wide_cols(b)].astype(F32)
        finish(total, dm, 1, row_block(b), pl.ds(0, 512))

    stores[0].start()

    far, near, _ = dn_copies(0)
    far.wait_send()
    pl.when(cross == 1)(near.wait_send)
    for hops in rings:
        for hop in hops:
            hop.wait_send()
    for chunk in range(4):
        g_copy(chunk).wait_send()
    settle(buf_a.at[pl.ds(0, 2 * GROUP - 2)], dd_send)
    settle(buf_b.at[pl.ds(0, 2 * GROUP - 2)], du_send)
    for store in stores:
        store.wait()


def shards(
    activations,
    cotangent,
    token_ids,
    path_table,
    up_master,
    down_master,
    up_momentum,
    down_momentum,
    up_first,
    up_second,
    down_first,
    down_second,
):
    anywhere = pl.BlockSpec(memory_space=pl.ANY)
    smem = pl.BlockSpec(memory_space=pltpu.SMEM)
    vmem = pl.BlockSpec(memory_space=pltpu.VMEM)
    dma = pltpu.SemaphoreType.DMA
    up_mean, down_mean = pl.pallas_call(
        kernel,
        out_shape=[jax.ShapeDtypeStruct(array.shape, F32) for array in (up_master, down_master)],
        in_specs=[smem, vmem] + [anywhere] * 8,
        out_specs=[anywhere] * 2,
        scratch_shapes=[
            pltpu.VMEM((C, 16, HALF_F), F32),
            pltpu.VMEM((C, 64, HALF_D), F32),
            *[pltpu.VMEM((C, 16, HALF_F), BF16)] * 8,
            *[pltpu.VMEM((C, 64, HALF_D), BF16)] * 8,
            pltpu.VMEM((C, 64, HALF_D), BF16),
            pltpu.VMEM((2 * GROUP, 16, HALF_F), BF16),
            pltpu.VMEM((2 * GROUP, 64, HALF_D), BF16),
            pltpu.VMEM((4, 2, 8, 16, HALF_F), BF16),
            pltpu.VMEM((2, GROUP, 64, HALF_D), BF16),
            pltpu.VMEM((2, GROUP, 16, HALF_F), BF16),
            pltpu.VMEM((2, GROUP, 64, HALF_D), BF16),
            pltpu.VMEM((HALF_F, HALF_D), BF16),
            pltpu.VMEM((HALF_F, HALF_D), BF16),
            pltpu.VMEM((HALF_F, HALF_D), BF16),
            pltpu.VMEM((2 * TOK, D), BF16),
            pltpu.VMEM((D, 2 * TOK), BF16),
            pltpu.VMEM((2 * TOK, D), BF16),
            pltpu.VMEM((2, 8, 128), F32),
            pltpu.SMEM((2 * C,), jnp.int32),
            pltpu.VMEM((2 * TOK, HALF_F), BF16),
            pltpu.VMEM((2, 2 * TOK, 256), F32),
            pltpu.VMEM((2, 2 * TOK, 256), BF16),
            pltpu.VMEM((2, 256, 512), F32),
            pltpu.VMEM((3, 2, 1024, 512), BF16),
            pltpu.VMEM((C, 16, HALF_F), BF16),
            pltpu.VMEM((C, 16, HALF_F), BF16),
            pltpu.VMEM((C, 64, HALF_D), BF16),
            pltpu.VMEM((C, 64, HALF_D), BF16),
            pltpu.VMEM((GROUP * 16, C * 16), F32),
            pltpu.VMEM((C * 16, GROUP * 16), BF16),
            pltpu.VMEM((C * 16, GROUP * 16), BF16),
            dma((4,)),
            dma((3, 2)),
            dma((2,)),
            dma((6,)),
            dma((6,)),
            dma((4, 4)),
            dma((4, 4)),
            dma((2,)),
            dma((2,)),
            dma,
            dma,
            dma,
            dma,
            dma((4,)),
            dma((4,)),
            dma,
            dma((2,)),
            dma,
            dma((2,)),
        ],
        compiler_params=pltpu.CompilerParams(
            collective_id=0, has_side_effects=True, vmem_limit_bytes=62 * 1024 * 1024
        ),
        cost_estimate=pl.CostEstimate(flops=12_884_901_888, bytes_accessed=30_000_000, transcendentals=1_572_864),
    )(
        path_table,
        token_ids,
        activations[0],
        cotangent[0],
        up_master,
        down_master,
        up_first[0],
        up_second[0],
        down_first[0],
        down_second[0],
    )
    new_up_momentum = 0.9 * up_momentum + up_mean
    new_down_momentum = 0.9 * down_momentum + down_mean
    new_up_master = up_master - 0.7 * (up_mean + 0.9 * new_up_momentum)
    new_down_master = down_master - 0.7 * (down_mean + 0.9 * new_down_momentum)
    return (new_up_master, new_down_master, new_up_momentum, new_down_momentum)


def solution(mesh):
    placed = (
        P("path", "dp", None),
        P("path", "dp", None),
        P("path", "dp"),
        P(),
        P(None, "path", "dp"),
        P(None, "path", "dp"),
        P(None, "path", "dp"),
        P(None, "path", "dp"),
        P("path", None, "dp"),
        P("path", None, "dp"),
        P("path", None, "dp"),
        P("path", None, "dp"),
    )
    return jax.shard_map(
        shards,
        mesh=mesh,
        in_specs=placed,
        out_specs=(
            P(None, "path", "dp"),
            P(None, "path", "dp"),
            P(None, "path", "dp"),
            P(None, "path", "dp"),
        ),
        check_vma=False,
    )
```

time: 250 us -> 278 us (1.11)
  the two profiles are of different devices: /device:TPU:18 before, /device:TPU:6 now
where the time goes in v6:
time: 278 us
  Pallas kernels  270 us (97%)
  other arithmetic  5.12 us (2%)
    pallas_call x1, Pallas kernels, shards(): pl.pallas_call(kernel, out_shape=[jax.ShapeDtypeStruct(array.shape, F32)...  270 us

profile of v6, /device:TPU:6, one launch (start us, length us, event | category | flops | bytes accessed | tf_op | source)
XLA Modules:
  0.0 277.5 jit_solution(18335910094495108132)
XLA Ops:
  0.6 1.4 copy.16.table
  2.0 0.0 copy-start
  2.0 270.3 %shard_map.147 = (f32[8,16,2048]{2,1,0:T(8,128)}, f32[8,64,512]{2,1,0:T(8,128)}) custom-call(s32[64,2]{1,0:T(8,128)} %copy.16.table, s32[1,384]{1,0:T(1,128)} %ids.1, bf16[384,1024]{1,0:T(8,128)(2,1)} %bitcast.10, bf16[384,1024]{1,0:T(8,128)(2,1)} %bitcast.11, f32[8,16,2048]{2,1,0:T(8,128)} %um_in.1, f32[8,64,512]{2,1,0:T(8,128)} %dm_in.1, ...), custom_call_target="tpu_custom_call" | custom-call | flops 12884901888 | bytes 30000000 | tf_op jit(solution)/shard_map/pallas_call | solution.py:604
  272.3 0.0 copy-start.1
  272.4 0.0 copy-start.2
  272.4 0.0 copy-start.3
  272.4 0.0 copy-done
  272.4 3.4 %multiply_subtract_fusion.1 = (f32[8,16,2048]{2,1,0:T(8,128)}, f32[8,16,2048]{2,1,0:T(8,128)}) fusion(f32[8,16,2048]{2,1,0:T(8,128)S(1)} %copy-done, f32[8,16,2048]{2,1,0:T(8,128)} %get-tuple-element.6, f32[8,16,2048]{2,1,0:T(8,128)} %param.18), kind=kLoop, calls=%fused_computation.2 | loop fusion | flops 1572864 | bytes 5242880 | tf_op jit(solution)/shard_map/sub | solution.py:679
  275.8 0.0 copy-done.1
  275.8 0.0 copy-done.2
  275.8 0.0 copy-done.3
  275.8 1.7 multiply_subtract_fusion
Async XLA Ops:
  2.0 270.4 %copy-start = (f32[8,16,2048]{2,1,0:T(8,128)S(1)}, f32[8,16,2048]{2,1,0:T(8,128)}, u32[]{:S(2)}) copy-start(f32[8,16,2048]{2,1,0:T(8,128)} %um_in.1) | copy-start | bytes 3145732
  272.3 3.5 %copy-start.1 = (f32[8,64,512]{2,1,0:T(8,128)S(1)}, f32[8,64,512]{2,1,0:T(8,128)}, u32[]{:S(2)}) copy-start(f32[8,64,512]{2,1,0:T(8,128)} %dm_in.1) | copy-start | bytes 3145732
  272.4 3.5 %copy-start.2 = (f32[8,64,512]{2,1,0:T(8,128)S(1)}, f32[8,64,512]{2,1,0:T(8,128)}, u32[]{:S(2)}) copy-start(f32[8,64,512]{2,1,0:T(8,128)} %param.19) | copy-start | bytes 3145732
  272.4 3.4 %copy-start.3 = (f32[8,64,512]{2,1,0:T(8,128)S(1)}, f32[8,64,512]{2,1,0:T(8,128)}, u32[]{:S(2)}) copy-start(f32[8,64,512]{2,1,0:T(8,128)} %get-tuple-element.7) | copy-start | bytes 3145732

commit v7 on v6

--- a/solution.py
+++ b/solution.py
@@ -107,8 +107,6 @@
         for kind in range(2):
             settle(mom.at[slot, kind], mom_sem.at[slot, kind])
 
-    for turn_no in range(3):
-        fetch(turn_no)
 
     cross = lax.rem(lax.div(x, 2) + here, 2)
     barrier = pltpu.get_barrier_semaphore()
@@ -329,6 +327,9 @@
 
     lax.fori_loop(0, 12, scale_rows, 0)
 
+    for turn_no in range(3):
+        fetch(turn_no)
+
     settle(wup, wu_recv)
     mine_cols = pl.ds(pl.multiple_of(here * HALF_D, HALF_D), HALF_D)
     their_cols = pl.ds(pl.multiple_of(there * HALF_D, HALF_D), HALF_D)
@@ -446,33 +447,25 @@
         def _():
             pltpu.make_async_copy(buf_b.at[row], rup.at[side, group], du_recv.at[side]).start()
 
-    def up_step(step, even):
-        x_ = lax.rem(x + lax.rem(2 + 3 * step, 4), 4)
-        slot = lax.rem(2 + even, 3)
+    def up_step(turn_no):
+        x_ = up_block[order[turn_no] - 4]
+        slot = turn_no % 3
         lhs = nrm_t[pl.ds(pl.multiple_of(x_ * 256, 256), 256), :]
+
+        def up_grad(b):
+            wide_b[b % 2] = jnp.dot(lhs, gp[:, pl.ds(b * 512, 512)], preferred_element_type=F32)
+
+        up_grad(0)
         await_moments(slot)
-
-        def up_grad(b, half):
-            cols = pl.ds(pl.multiple_of(b * 512, 512), 512)
-            wide_b[half] = jnp.dot(lhs, gp[:, cols], preferred_element_type=F32)
-
-        def strips(b, half):
+        for b in range(4):
+            if b < 3:
+                up_grad(b + 1)
             for i in range(16):
-                rows = pl.ds(pl.multiple_of(b * 256 + i * 16, 16), 16)
-                grad = wide_b[half, pl.ds(i * 16, 16), :] * UP_SCALE
+                rows = pl.ds(b * 256 + i * 16, 16)
+                grad = wide_b[b % 2, pl.ds(i * 16, 16), :] * UP_SCALE
                 delta = step_direction(grad, mom[slot, 0, rows, :], mom[slot, 1, rows, :])
-                buf_b[x_ * 16 + i, pl.ds(pl.multiple_of(b * 16, 16), 16), :] = delta
-
-        up_grad(0, 0)
-
-        def pair(n, _):
-            up_grad(2 * n + 1, 1)
-            strips(2 * n, 0)
-            up_grad(lax.rem(2 * n + 2, 4), 0)
-            strips(2 * n + 1, 1)
-            return 0
-
-        lax.fori_loop(0, 2, pair, 0)
+                buf_b[x_ * 16 + i, pl.ds(b * 16, 16), :] = delta
+        fetch(turn_no + 3)
 
         def send(k, _):
             send_up_delta(x_, zc_at(k), lax.rem(other_yl + lax.div(k, 8), 2))
@@ -480,46 +473,25 @@
 
         lax.fori_loop(0, 16, send, 0)
 
-    def early(n, _):
-        up_step(n, n)
-        pl.when(n == 0)(lambda: fetch(5))
-        pl.when(n == 1)(lambda: fetch(6))
-        return 0
-
-    def late(n, _):
-        up_step(n + 2, n)
-        return 0
-
-    lax.fori_loop(0, 2, early, 0)
+    up_step(2)
+    up_step(3)
     down_delta(4)
     send_down_delta(2, other_yl)
     send_down_delta(2, yl)
-    lax.fori_loop(0, 2, late, 0)
+    up_step(5)
+    up_step(6)
     down_delta(7)
     for side in (other_yl, yl):
         send_down_delta(1, side)
         send_down_delta(3, side)
 
-    def wide_cols(b):
-        return pl.ds(pl.multiple_of(b * 512, 512), 512)
-
-    def row_block(b):
-        return pl.ds(pl.multiple_of(b * 16, 16), 16)
-
     def down_sum(side, b):
-        block = rdn[side, :, :, wide_cols(b)].reshape(GROUP * 16, 512)
+        block = rdn[side, :, :, pl.ds(b * 512, 512)].reshape(GROUP * 16, 512)
         return jnp.dot(pick_dn[...], block, preferred_element_type=F32).reshape(C, 16, 512)
 
     def up_sum(side, b):
-        block = rup[side, :, row_block(b), :].reshape(GROUP * 16, 512)
+        block = rup[side, :, pl.ds(b * 16, 16), :].reshape(GROUP * 16, 512)
         return jnp.dot(pick_up[...], block, preferred_element_type=F32).reshape(C, 16, 512)
-
-    def four(body):
-        def one(b, _):
-            body(b)
-            return 0
-
-        lax.fori_loop(0, 4, one, 0)
 
     def finish(total, master, level, rows, cols):
         for m in range(C):
@@ -534,39 +506,29 @@
         pltpu.make_async_copy(src, dst, out_sem.at[i]) for i, (src, dst) in enumerate([(dm, dm_out), (um, um_out)])
     ]
     settle(rup.at[other_yl], du_recv.at[other_yl])
-
-    @four
-    def _(b):
-        pup_send[:, row_block(b), :] = up_sum(other_yl, b).astype(BF16)
-
+    for b in range(4):
+        pup_send[:, pl.ds(b * 16, 16), :] = up_sum(other_yl, b).astype(BF16)
     up_part = remote(pup_send, pup_recv, y_send.at[5], y_recv.at[5], mate, here)
     up_part.start()
     settle(rup.at[yl], du_recv.at[yl])
     up_part.wait()
-
-    @four
-    def _(b):
-        total = up_sum(yl, b) + pup_recv[:, row_block(b), :].astype(F32)
-        finish(total, um, 0, pl.ds(0, 16), wide_cols(b))
-
+    for b in range(4):
+        rows = pl.ds(b * 16, 16)
+        total = up_sum(yl, b) + pup_recv[:, rows, :].astype(F32)
+        finish(total, um, 0, pl.ds(0, 16), pl.ds(b * 512, 512))
     stores[1].start()
 
     settle(rdn.at[other_yl], dd_recv.at[other_yl])
-
-    @four
-    def _(b):
-        pdn_send[:, :, wide_cols(b)] = down_sum(other_yl, b).astype(BF16)
-
+    for b in range(4):
+        pdn_send[:, :, pl.ds(b * 512, 512)] = down_sum(other_yl, b).astype(BF16)
     dn_part = remote(pdn_send, pdn_recv, y_send.at[4], y_recv.at[4], mate, here)
     dn_part.start()
     settle(rdn.at[yl], dd_recv.at[yl])
     dn_part.wait()
-
-    @four
-    def _(b):
-        total = down_sum(yl, b) + pdn_recv[:, :, wide_cols(b)].astype(F32)
-        finish(total, dm, 1, row_block(b), pl.ds(0, 512))
-
+    for b in range(4):
+        cols = pl.ds(b * 512, 512)
+        total = down_sum(yl, b) + pdn_recv[:, :, cols].astype(F32)
+        finish(total, dm, 1, pl.ds(b * 16, 16), pl.ds(0, 512))
     stores[0].start()
 
     far, near, _ = dn_copies(0)

time: 278 us -> 276 us (level)
  Pallas kernels: 270 us -> 267 us
    pallas_call x1, Pallas kernels: 270 us -> 267 us  [shards(): pl.pallas_call(kernel, out_shape=[jax.ShapeDtypeStruct(array.shape, F32)...]
where the time goes in v7:
time: 276 us; the launch traced here: 274 us
  Pallas kernels  267 us (97%)
  other arithmetic  5.12 us (2%)
    pallas_call x1, Pallas kernels, shards(): pl.pallas_call(kernel, out_shape=[jax.ShapeDtypeStruct(array.shape, F32)...  267 us

profile of v7, /device:TPU:6, one launch (start us, length us, event | category | flops | bytes accessed | tf_op | source)
XLA Modules:
  0.0 274.4 jit_solution(6217246608313943735)
XLA Ops:
  0.6 1.4 copy.16.table
  2.0 0.0 copy-start
  2.0 267.2 %shard_map.147 = (f32[8,16,2048]{2,1,0:T(8,128)}, f32[8,64,512]{2,1,0:T(8,128)}) custom-call(s32[64,2]{1,0:T(8,128)} %copy.16.table, s32[1,384]{1,0:T(1,128)} %ids.1, bf16[384,1024]{1,0:T(8,128)(2,1)} %bitcast.10, bf16[384,1024]{1,0:T(8,128)(2,1)} %bitcast.11, f32[8,16,2048]{2,1,0:T(8,128)} %um_in.1, f32[8,64,512]{2,1,0:T(8,128)} %dm_in.1, ...), custom_call_target="tpu_custom_call" | custom-call | flops 12884901888 | bytes 30000000 | tf_op jit(solution)/shard_map/pallas_call | solution.py:566
  269.3 0.0 copy-start.1
  269.3 0.0 copy-start.2
  269.3 0.0 copy-start.3
  269.3 0.0 copy-done
  269.3 3.4 %multiply_subtract_fusion.1 = (f32[8,16,2048]{2,1,0:T(8,128)}, f32[8,16,2048]{2,1,0:T(8,128)}) fusion(f32[8,16,2048]{2,1,0:T(8,128)S(1)} %copy-done, f32[8,16,2048]{2,1,0:T(8,128)} %get-tuple-element.6, f32[8,16,2048]{2,1,0:T(8,128)} %param.18), kind=kLoop, calls=%fused_computation.2 | loop fusion | flops 1572864 | bytes 5242880 | tf_op jit(solution)/shard_map/sub | solution.py:641
  272.7 0.0 copy-done.1
  272.7 0.0 copy-done.2
  272.7 0.0 copy-done.3
  272.7 1.7 multiply_subtract_fusion
Async XLA Ops:
  2.0 267.3 %copy-start = (f32[8,16,2048]{2,1,0:T(8,128)S(1)}, f32[8,16,2048]{2,1,0:T(8,128)}, u32[]{:S(2)}) copy-start(f32[8,16,2048]{2,1,0:T(8,128)} %um_in.1) | copy-start | bytes 3145732
  269.3 3.5 %copy-start.1 = (f32[8,64,512]{2,1,0:T(8,128)S(1)}, f32[8,64,512]{2,1,0:T(8,128)}, u32[]{:S(2)}) copy-start(f32[8,64,512]{2,1,0:T(8,128)} %dm_in.1) | copy-start | bytes 3145732
  269.3 3.5 %copy-start.2 = (f32[8,64,512]{2,1,0:T(8,128)S(1)}, f32[8,64,512]{2,1,0:T(8,128)}, u32[]{:S(2)}) copy-start(f32[8,64,512]{2,1,0:T(8,128)} %param.19) | copy-start | bytes 3145732
  269.3 3.4 %copy-start.3 = (f32[8,64,512]{2,1,0:T(8,128)S(1)}, f32[8,64,512]{2,1,0:T(8,128)}, u32[]{:S(2)}) copy-start(f32[8,64,512]{2,1,0:T(8,128)} %get-tuple-element.7) | copy-start | bytes 3145732

commit v8 on v3

--- a/solution.py
+++ b/solution.py
@@ -331,8 +331,12 @@
         lax.fori_loop(0, 8, send, 0)
 
     settle(buf_a.at[pl.ds(0, GROUP - 1)], wu_send.at[1])
+    down_delta(0)
+    down_delta(1)
+    settle(buf_b.at[pl.ds(0, 2 * GROUP - 2)], wd_send)
     for turn_no in range(4):
-        down_delta(turn_no)
+        if turn_no >= 2:
+            down_delta(turn_no)
         send_down_delta(turn_no, other_yl)
         send_down_delta(turn_no, yl)
 
@@ -348,7 +352,6 @@
         return 0
 
     lax.fori_loop(0, 8, hidden_grad, 0)
-    settle(buf_b.at[pl.ds(0, 2 * GROUP - 2)], wd_send)
 
     def send_up_delta(x_, zc_, side):
         row = x_ * 16 + side * 8 + zc_
@@ -384,21 +387,18 @@
                 buf_b[x_ * 16 + i, pl.ds(b * 16, 16), :] = delta
         fetch(turn_no + 2)
 
-        def send(k, _):
-            send_up_delta(x_, zc_at(k), other_yl)
-            return 0
-
-        lax.fori_loop(0, 8, send, 0)
-
     for turn_no in range(4, 8):
         up_step(turn_no)
 
-    def send_rest(k, _):
-        x_, zc_ = peer(lax.rem(k * 11, GROUP))
-        send_up_delta(x_, zc_, yl)
-        return 0
-
-    lax.fori_loop(0, GROUP, send_rest, 0)
+    settle(buf_a.at[pl.ds(0, 2 * GROUP - 2)], dd_send)
+    for side in (other_yl, yl):
+
+        def send_side(k, _, side=side):
+            x_, zc_ = peer(lax.rem(k * 11, GROUP))
+            send_up_delta(x_, zc_, side)
+            return 0
+
+        lax.fori_loop(0, GROUP, send_side, 0)
 
     lane = lax.broadcasted_iota(jnp.int32, (16, C * 16), 1)
     same_row = (lane & 15) == lax.broadcasted_iota(jnp.int32, (16, C * 16), 0)
@@ -475,7 +475,6 @@
 
     for chunk in range(4):
         g_copy(chunk).wait_send()
-    settle(buf_a.at[pl.ds(0, 2 * GROUP - 2)], dd_send)
     settle(buf_b.at[pl.ds(0, 2 * GROUP - 2)], du_send)
     for store in stores:
         store.wait()

time: 249 us -> 286 us (1.15)
  the two profiles are of different devices: /device:TPU:6 before, /device:TPU:35 now
where the time goes in v8:
time: 286 us
  Pallas kernels  278 us (97%)
  other arithmetic  5.12 us (2%)
    pallas_call x1, Pallas kernels, shards(): pl.pallas_call(kernel, out_shape=[jax.ShapeDtypeStruct(array.shape, F32)...  278 us

profile of v8, /device:TPU:35, one launch (start us, length us, event | category | flops | bytes accessed | tf_op | source)
XLA Modules:
  0.0 285.6 jit_solution(3180816727953413459)
XLA Ops:
  0.6 1.4 copy.16.table
  2.0 0.0 copy-start
  2.0 278.4 %shard_map.147 = (f32[8,16,2048]{2,1,0:T(8,128)}, f32[8,64,512]{2,1,0:T(8,128)}) custom-call(s32[64,2]{1,0:T(8,128)} %copy.16.table, s32[1,384]{1,0:T(1,128)} %ids.1, bf16[384,1024]{1,0:T(8,128)(2,1)} %bitcast.10, bf16[384,1024]{1,0:T(8,128)(2,1)} %bitcast.11, f32[8,16,2048]{2,1,0:T(8,128)} %um_in.1, f32[8,64,512]{2,1,0:T(8,128)} %dm_in.1, ...), custom_call_target="tpu_custom_call" | custom-call | flops 12884901888 | bytes 30000000 | tf_op jit(solution)/shard_map/pallas_call | solution.py:501
  280.4 0.0 copy-start.1
  280.4 0.0 copy-start.2
  280.4 0.0 copy-start.3
  280.5 0.0 copy-done
  280.5 3.4 %multiply_subtract_fusion.1 = (f32[8,16,2048]{2,1,0:T(8,128)}, f32[8,16,2048]{2,1,0:T(8,128)}) fusion(f32[8,16,2048]{2,1,0:T(8,128)S(1)} %copy-done, f32[8,16,2048]{2,1,0:T(8,128)} %get-tuple-element.6, f32[8,16,2048]{2,1,0:T(8,128)} %param.18), kind=kLoop, calls=%fused_computation.2 | loop fusion | flops 1572864 | bytes 5242880 | tf_op jit(solution)/shard_map/sub | solution.py:577
  283.9 0.0 copy-done.1
  283.9 0.0 copy-done.2
  283.9 0.0 copy-done.3
  283.9 1.7 multiply_subtract_fusion
Async XLA Ops:
  2.0 278.4 %copy-start = (f32[8,16,2048]{2,1,0:T(8,128)S(1)}, f32[8,16,2048]{2,1,0:T(8,128)}, u32[]{:S(2)}) copy-start(f32[8,16,2048]{2,1,0:T(8,128)} %um_in.1) | copy-start | bytes 3145732
  280.4 3.5 %copy-start.1 = (f32[8,64,512]{2,1,0:T(8,128)S(1)}, f32[8,64,512]{2,1,0:T(8,128)}, u32[]{:S(2)}) copy-start(f32[8,64,512]{2,1,0:T(8,128)} %dm_in.1) | copy-start | bytes 3145732
  280.4 3.5 %copy-start.2 = (f32[8,64,512]{2,1,0:T(8,128)S(1)}, f32[8,64,512]{2,1,0:T(8,128)}, u32[]{:S(2)}) copy-start(f32[8,64,512]{2,1,0:T(8,128)} %param.19) | copy-start | bytes 3145732
  280.4 3.4 %copy-start.3 = (f32[8,64,512]{2,1,0:T(8,128)S(1)}, f32[8,64,512]{2,1,0:T(8,128)}, u32[]{:S(2)}) copy-start(f32[8,64,512]{2,1,0:T(8,128)} %get-tuple-element.7) | copy-start | bytes 3145732

commit v9 on v3

--- a/solution.py
+++ b/solution.py
@@ -331,7 +331,7 @@
         lax.fori_loop(0, 8, send, 0)
 
     settle(buf_a.at[pl.ds(0, GROUP - 1)], wu_send.at[1])
-    for turn_no in range(4):
+    for turn_no in range(2):
         down_delta(turn_no)
         send_down_delta(turn_no, other_yl)
         send_down_delta(turn_no, yl)
@@ -349,6 +349,10 @@
 
     lax.fori_loop(0, 8, hidden_grad, 0)
     settle(buf_b.at[pl.ds(0, 2 * GROUP - 2)], wd_send)
+    for turn_no in range(2, 4):
+        down_delta(turn_no)
+        send_down_delta(turn_no, other_yl)
+        send_down_delta(turn_no, yl)
 
     def send_up_delta(x_, zc_, side):
         row = x_ * 16 + side * 8 + zc_
@@ -573,9 +577,13 @@
         down_first[0],
         down_second[0],
     )
-    new_up_momentum = 0.9 * up_momentum + up_mean
+    flat = (C * 16, HALF_F)
+    up_mean = up_mean.reshape(flat)
+    new_up_momentum = 0.9 * up_momentum.reshape(flat) + up_mean
+    new_up_master = up_master.reshape(flat) - 0.7 * (up_mean + 0.9 * new_up_momentum)
+    new_up_momentum = new_up_momentum.reshape(up_momentum.shape)
+    new_up_master = new_up_master.reshape(up_master.shape)
     new_down_momentum = 0.9 * down_momentum + down_mean
-    new_up_master = up_master - 0.7 * (up_mean + 0.9 * new_up_momentum)
     new_down_master = down_master - 0.7 * (down_mean + 0.9 * new_down_momentum)
     return (new_up_master, new_down_master, new_up_momentum, new_down_momentum)
 

time: 249 us -> 273 us (1.096)
  the two profiles are of different devices: /device:TPU:6 before, /device:TPU:82 now
where the time goes in v9:
time: 273 us
  Pallas kernels  266 us (97%)
  other arithmetic  5.12 us (2%)
    pallas_call x1, Pallas kernels, shards(): pl.pallas_call(kernel, out_shape=[jax.ShapeDtypeStruct(array.shape, F32)...  266 us

profile of v9, /device:TPU:82, one launch (start us, length us, event | category | flops | bytes accessed | tf_op | source)
XLA Modules:
  0.0 273.1 jit_solution(6878296459345118279)
XLA Ops:
  0.6 1.4 copy.16.table
  2.0 0.0 copy-start
  2.0 265.9 %shard_map.147 = (f32[8,16,2048]{2,1,0:T(8,128)}, f32[8,64,512]{2,1,0:T(8,128)}) custom-call(s32[64,2]{1,0:T(8,128)} %copy.16.table, s32[1,384]{1,0:T(1,128)} %ids.1, bf16[384,1024]{1,0:T(8,128)(2,1)} %bitcast.10, bf16[384,1024]{1,0:T(8,128)(2,1)} %bitcast.11, f32[8,16,2048]{2,1,0:T(8,128)} %um_in.1, f32[8,64,512]{2,1,0:T(8,128)} %dm_in.1, ...), custom_call_target="tpu_custom_call" | custom-call | flops 12884901888 | bytes 30000000 | tf_op jit(solution)/shard_map/pallas_call | solution.py:506
  267.9 0.0 copy-start.1
  267.9 0.0 copy-start.2
  267.9 0.0 copy-start.3
  267.9 0.0 copy-done
  267.9 3.4 %multiply_subtract_fusion.1 = (f32[8,16,2048]{2,1,0:T(8,128)}, f32[8,16,2048]{2,1,0:T(8,128)}) fusion(f32[8,16,2048]{2,1,0:T(8,128)S(1)} %copy-done, f32[8,16,2048]{2,1,0:T(8,128)} %get-tuple-element.6, f32[8,16,2048]{2,1,0:T(8,128)} %param.18), kind=kLoop, calls=%fused_computation.2 | loop fusion | flops 1572864 | bytes 5242880 | tf_op jit(solution)/shard_map/sub | solution.py:583
  271.3 0.0 copy-done.1
  271.3 0.0 copy-done.2
  271.4 0.0 copy-done.3
  271.4 1.7 multiply_subtract_fusion
Async XLA Ops:
  2.0 265.9 %copy-start = (f32[8,16,2048]{2,1,0:T(8,128)S(1)}, f32[8,16,2048]{2,1,0:T(8,128)}, u32[]{:S(2)}) copy-start(f32[8,16,2048]{2,1,0:T(8,128)} %um_in.1) | copy-start | bytes 3145732
  267.9 3.5 %copy-start.1 = (f32[8,64,512]{2,1,0:T(8,128)S(1)}, f32[8,64,512]{2,1,0:T(8,128)}, u32[]{:S(2)}) copy-start(f32[8,64,512]{2,1,0:T(8,128)} %dm_in.1) | copy-start | bytes 3145732
  267.9 3.5 %copy-start.2 = (f32[8,64,512]{2,1,0:T(8,128)S(1)}, f32[8,64,512]{2,1,0:T(8,128)}, u32[]{:S(2)}) copy-start(f32[8,64,512]{2,1,0:T(8,128)} %param.19) | copy-start | bytes 3145732
  267.9 3.4 %copy-start.3 = (f32[8,64,512]{2,1,0:T(8,128)S(1)}, f32[8,64,512]{2,1,0:T(8,128)}, u32[]{:S(2)}) copy-start(f32[8,64,512]{2,1,0:T(8,128)} %get-tuple-element.7) | copy-start | bytes 3145732
